TPU v7x, 32 devices: a whole 2x2x4 slice. The times are simulated.
32 devices in a mesh: row: 8 (over y, x, core), col: 4 (over z).
Axes of the slice: x: 2, y: 2, z: 4, core: 2. Of those that a mesh axis runs over, the one named last changes fastest.
Arguments:
- diag_blocks: bfloat16 [256, 128, 128], P(('row', 'col')), may hold values from -0.03 to 3, as said below
- off_blocks: bfloat16 [256, 6, 128, 128], P(('row', 'col')), may hold values from -0.375 to 0.375
- neighbors: int32 [256, 6], P(('row', 'col')), may hold values from -1 to 255, as said below
- levels: int32 [256], P(('row', 'col')), may hold values from 0 to 1, as said below
Outputs:
- pivot_inverse: bfloat16 [256, 128, 128], P(('row', 'col'))
- factor_blocks: bfloat16 [256, 6, 128, 128], P(('row', 'col'))
Inputs may be any that keep to these rules, and one draw needn't show every extreme that they name: `levels`: block row i lies on device number d = i // 8, where d = r * (number of devices along col) + c for the device with index r along row and index c along col. On each device the rows of level 0 come first; a device holds between 2 and 6 rows of level 0, and in every draw some device holds exactly 6 and some exactly 2. `neighbors`: A live slot names a row of the other level. Slot 0 names a row on the device whose row index is one higher, slot 1 one lower, slot 2 on the device whose col index is one higher, slot 3 one lower, slots 4 and 5 on the same device. If row i names row j in slot k, row j names row i in slot (1, 0, 3, 2, 5, 4)[k]. `diag_blocks`: diagonal entries from 1 to 3; off-diagonal entries of either sign, each row's sum of their magnitudes under 0.9 times that row's diagonal entry.
All inputs are finite; a program needn't handle non-finite values.
Results may differ from a plain program's by a relative error of at most 0.0053.
Values may be sent and summed in bfloat16 or wider, within the bound.
No kernel may reach another device: no remote copies, remote signals or barrier semaphores. Data moves between devices by JAX's collectives and lax.ppermute only.
A program may use at most 64 MiB of HBM per device.

v0:
```python
import jax
import jax.numpy as jnp
from jax import lax
from jax.sharding import PartitionSpec as P

NS_STEPS = 4


MIRROR = (1, 0, 3, 2, 5, 4)


def padded(value, sides, width):
    for axis, dim in sides:
        size, length = (lax.axis_size(axis), value.shape[dim])
        up = [(i, (i + 1) % size) for i in range(size - 1)]
        down = [(j, i) for i, j in up]
        last = lax.slice_in_dim(value, length - width, length, axis=dim)
        initial = lax.slice_in_dim(value, 0, width, axis=dim)
        before = lax.ppermute(last, axis, up)
        after = lax.ppermute(initial, axis, down)
        value = jnp.concatenate([before, value, after], axis=dim)
    return value


def approx_inverse(matrix):
    magnitude = jnp.abs(matrix)
    column_norm = jnp.max(jnp.sum(magnitude, axis=1), axis=1)
    row_norm = jnp.max(jnp.sum(magnitude, axis=2), axis=1)
    iterate = jnp.swapaxes(matrix, 1, 2) / (column_norm * row_norm)[:, None, None]
    for step_index in range(NS_STEPS):
        product = jnp.einsum("nij,njk->nik", matrix, iterate, precision=lax.Precision.HIGHEST)
        iterate = 2.0 * iterate - jnp.einsum(
            "nij,njk->nik", iterate, product, precision=lax.Precision.HIGHEST
        )
    return iterate


def shards(diag_blocks, off_blocks, neighbors, levels):
    rows_here = diag_blocks.shape[0]
    capacity = 3 * rows_here // 4
    slot_count = off_blocks.shape[1]
    block_size = diag_blocks.shape[1]
    active = neighbors >= 0
    first_inverse = approx_inverse(diag_blocks[:capacity].astype(jnp.float32)).astype(jnp.bfloat16)
    upper_rows = jnp.einsum(
        "nij,nkjl->nkil", first_inverse, off_blocks[:capacity], preferred_element_type=jnp.float32
    )
    upper_rows = jnp.where(active[:capacity, :, None, None], upper_rows, 0.0).astype(jnp.bfloat16)

    def paired(source_blocks, source_inverse, slot_index):
        return jnp.stack((source_blocks[:, slot_index], source_inverse), axis=1)

    packed = jnp.concatenate([upper_rows, first_inverse[:, None]], axis=1)
    extended = padded(packed[None, None], (("row", 0), ("col", 1)), 1)
    sources = [extended[2, 1], extended[0, 1], extended[1, 2], extended[1, 0], packed, packed]
    tables = [
        paired(sources[slot_index], sources[slot_index][:, slot_count], MIRROR[slot_index])
        for slot_index in range(slot_count)
    ]
    table = jnp.stack(tables, axis=0)
    start = rows_here - capacity
    later_named = neighbors[start:]
    later_active = active[start:]
    local_rows = jnp.clip(jnp.where(later_active, later_named % rows_here, 0), 0, capacity - 1)
    picked = table[jnp.arange(slot_count)[None, :], local_rows]
    lower_blocks = jnp.where(
        later_active[:, :, None, None], off_blocks[start:], jnp.zeros((), jnp.bfloat16)
    )
    lower_factor = jnp.einsum(
        "qkij,qkjl->qkil", lower_blocks, picked[:, :, 1], preferred_element_type=jnp.float32
    ).astype(jnp.bfloat16)
    schur = jnp.einsum(
        "qkij,qkjl->qil", lower_blocks, picked[:, :, 0], preferred_element_type=jnp.float32
    )
    second_inverse = approx_inverse(diag_blocks[start:].astype(jnp.float32) - schur).astype(
        jnp.bfloat16
    )
    early = levels == 0
    pivot_first = jnp.concatenate(
        [first_inverse, jnp.zeros((start, block_size, block_size), jnp.bfloat16)], axis=0
    )
    pivot_second = jnp.concatenate(
        [jnp.zeros((start, block_size, block_size), jnp.bfloat16), second_inverse], axis=0
    )
    pivot_inverse = jnp.where(early[:, None, None], pivot_first, pivot_second)
    factor_first = jnp.concatenate(
        [upper_rows, jnp.zeros((start, slot_count, block_size, block_size), jnp.bfloat16)], axis=0
    )
    factor_second = jnp.concatenate(
        [jnp.zeros((start, slot_count, block_size, block_size), jnp.bfloat16), lower_factor], axis=0
    )
    factor_blocks = jnp.where(early[:, None, None, None], factor_first, factor_second)
    return (pivot_inverse, factor_blocks)


def solution(mesh):
    in_specs = (
        P(("row", "col"), None, None),
        P(("row", "col"), None, None, None),
        P(("row", "col"), None),
        P(("row", "col")),
    )
    out_specs = (P(("row", "col"), None, None), P(("row", "col"), None, None, None))
    return jax.shard_map(shards, mesh=mesh, in_specs=in_specs, out_specs=out_specs, check_vma=False)
```

profile of v0, /device:TPU:28, one launch (start us, length us, event | category | flops | bytes accessed | tf_op | source)
XLA Modules:
  0.0 167.6 jit_solution(14672751580386746425)
XLA Ops:
  1.4 1.1 fusion.7
  2.7 1.6 fusion.17
  8.2 1.2 fusion.41
  10.3 2.8 %collective-permute-start = (bf16[1,1,6,7,128,128]{4,5,2,3,1,0:T(8,128)(2,1)S(1)}, bf16[1,1,6,7,128,128]{4,5,2,3,1,0:T(8,128)(2,1)S(1)}, u32[]{:S(2)}, u32[]{:S(2)}) collective-permute-start(bf16[1,1,6,7,128,128]{4,5,2,3,1,0:T(8,128)(2,1)S(1)} %maximum_bitcast_fusion), channel_id=1, source_target_pairs={{4,0},{8,4},{12,8},{16,12},{20,16},{24,20},{28,24},{5,1},{9,5},{13... | collective-permute-start | bytes 4128776 | tf_op jit(solution)/shard_map/ppermute | solution.py:20
  13.1 1.9 %collective-permute-start.1 = (bf16[1,1,6,7,128,128]{4,5,2,3,1,0:T(8,128)(2,1)S(1)}, bf16[1,1,6,7,128,128]{4,5,2,3,1,0:T(8,128)(2,1)S(1)}, u32[]{:S(2)}, u32[]{:S(2)}) collective-permute-start(bf16[1,1,6,7,128,128]{4,5,2,3,1,0:T(8,128)(2,1)S(1)} %maximum_bitcast_fusion), channel_id=1, source_target_pairs={{0,4},{4,8},{8,12},{12,16},{16,20},{20,24},{24,28},{1,5},{5,9},{9,... | collective-permute-start | bytes 4128776 | tf_op jit(solution)/shard_map/ppermute | solution.py:19
  15.0 26.6 %collective-permute-done = bf16[1,1,6,7,128,128]{4,5,2,3,1,0:T(8,128)(2,1)S(1)} collective-permute-done((bf16[1,1,6,7,128,128]{4,5,2,3,1,0:T(8,128)(2,1)S(1)}, bf16[1,1,6,7,128,128]{4,5,2,3,1,0:T(8,128)(2,1)S(1)}, u32[]{:S(2)}, u32[]{:S(2)}) %collective-permute-start) | collective-permute-done | bytes 1376288 | tf_op jit(solution)/shard_map/ppermute | solution.py:20
  41.6 3.1 %collective-permute-done.1 = bf16[1,1,6,7,128,128]{4,5,2,3,1,0:T(8,128)(2,1)S(1)} collective-permute-done((bf16[1,1,6,7,128,128]{4,5,2,3,1,0:T(8,128)(2,1)S(1)}, bf16[1,1,6,7,128,128]{4,5,2,3,1,0:T(8,128)(2,1)S(1)}, u32[]{:S(2)}, u32[]{:S(2)}) %collective-permute-start.1) | collective-permute-done | bytes 1376288 | tf_op jit(solution)/shard_map/ppermute | solution.py:19
  44.7 2.2 %pad_maximum_fusion = bf16[3,1,6,7,128,128]{4,5,2,3,1,0:T(8,128)(2,1)} fusion(bf16[1,1,6,7,128,128]{4,5,2,3,1,0:T(8,128)(2,1)S(1)} %collective-permute-done, bf16[1,1,6,7,128,128]{4,5,2,3,1,0:T(8,128)(2,1)S(1)} %maximum_bitcast_fusion, bf16[1,1,6,7,128,128]{4,5,2,3,1,0:T(8,128)(2,1)S(1)} %collective-permute-done.1), kind=kLoop, calls=%fused_computation.1 | loop fusion | flops 4128768 | bytes 8257536 | tf_op jit(solution)/shard_map/concatenate | solution.py:21
  46.8 4.3 %collective-permute-start.2 = (bf16[3,1,6,7,128,128]{4,5,2,3,1,0:T(8,128)(2,1)}, bf16[3,1,6,7,128,128]{4,5,2,3,1,0:T(8,128)(2,1)}, u32[]{:S(2)}, u32[]{:S(2)}) collective-permute-start(bf16[3,1,6,7,128,128]{4,5,2,3,1,0:T(8,128)(2,1)} %pad_maximum_fusion), channel_id=1, source_target_pairs={{1,0},{2,1},{3,2},{5,4},{6,5},{7,6},{9,8},{10,9},{11,10},{13,12},{... | collective-permute-start | bytes 12386312 | tf_op jit(solution)/shard_map/ppermute | solution.py:20
  51.2 1.5 collective-permute-start.3
  52.8 1.1 fusion.45
  55.4 81.7 %collective-permute-done.2 = bf16[3,1,6,7,128,128]{4,5,2,3,1,0:T(8,128)(2,1)} collective-permute-done((bf16[3,1,6,7,128,128]{4,5,2,3,1,0:T(8,128)(2,1)}, bf16[3,1,6,7,128,128]{4,5,2,3,1,0:T(8,128)(2,1)}, u32[]{:S(2)}, u32[]{:S(2)}) %collective-permute-start.2) | collective-permute-done | bytes 4128800 | tf_op jit(solution)/shard_map/ppermute | solution.py:20
  137.2 1.4 slice_bitcast_fusion.1
  138.6 4.6 %collective-permute-done.3 = bf16[3,1,6,7,128,128]{4,5,2,3,1,0:T(8,128)(2,1)} collective-permute-done((bf16[3,1,6,7,128,128]{4,5,2,3,1,0:T(8,128)(2,1)}, bf16[3,1,6,7,128,128]{4,5,2,3,1,0:T(8,128)(2,1)}, u32[]{:S(2)}, u32[]{:S(2)}) %collective-permute-start.3) | collective-permute-done | bytes 4128800 | tf_op jit(solution)/shard_map/ppermute | solution.py:19
  143.2 1.4 slice_bitcast_fusion
  147.9 4.3 %gather_fusion = bf16[36,2,128,128]{2,3,1,0:T(8,128)(2,1)} fusion(bf16[6,6,2,128,128]{3,4,1,2,0:T(8,128)(2,1)} %fusion.12, s32[36]{0:T(128)S(1)} %reshape.21), kind=kCustom, calls=%fused_computation | custom fusion | bytes 4718880 | tf_op jit(solution)/shard_map/gather | solution.py:65
  152.2 2.0 %abs_reduce_fusion = (f32[6,128]{1,0:T(8,128)S(1)}, f32[6,128]{1,0:T(8,128)S(1)}, f32[6,128,128]{2,1,0:T(8,128)S(1)}) fusion(bf16[6,6,128,128]{3,2,1,0:T(8,128)(2,1)S(1)} %copy-done.4, bf16[6,6,2,128,128]{3,4,2,1,0:T(8,128)(2,1)} %bitcast.93, bf16[8,128,128]{2,1,0:T(8,128)(2,1)S(1)} %copy-done.2), kind=kOutput, calls=%fused_computation.45 | convolution fusion | flops 151484928 | bytes 2955264 | tf_op jit(solution)/shard_map/qkij,qkjl->qil/dot_general | solution.py:72
  154.2 2.0 %convolution_convert_fusion = bf16[6,6,128,128]{2,3,0,1:T(8,128)(2,1)} fusion(bf16[6,6,128,128]{3,2,1,0:T(8,128)(2,1)S(1)} %copy-done.4, bf16[6,6,2,128,128]{3,4,2,1,0:T(8,128)(2,1)S(1)} %bitcast.94), kind=kOutput, calls=%fused_computation.4 | convolution fusion | flops 151584768 | bytes 3538944 | tf_op jit(solution)/shard_map/qkij,qkjl->qkil/dot_general | solution.py:69
  156.4 1.0 fusion.18
  158.3 0.9 fusion.48
  160.1 0.9 fusion.49
  161.8 0.9 fusion.50
  164.5 1.5 pad_select_fusion
  166.0 1.6 copy.56
  (51 shorter events, 15.2 us)
Async XLA Ops:
  0.6 3.7 %copy-start.2 = (bf16[8,128,128]{2,1,0:T(8,128)(2,1)S(1)}, bf16[8,128,128]{2,1,0:T(8,128)(2,1)}, u32[]{:S(2)}) copy-start(bf16[8,128,128]{2,1,0:T(8,128)(2,1)} %param.4) | copy-start | bytes 786436
  6.5 1.7 %copy-start = (bf16[8,6,128,128]{3,2,1,0:T(8,128)(2,1)S(1)}, bf16[8,6,128,128]{3,2,1,0:T(8,128)(2,1)}, u32[]{:S(2)}) copy-start(bf16[8,6,128,128]{3,2,1,0:T(8,128)(2,1)} %param.5) | copy-start | bytes 4718596
  10.3 42.4 %copy-start.5 = (s32[8,6]{1,0:T(8,128)S(1)}, s32[8,6]{1,0:T(8,128)}, u32[]{:S(2)}) copy-start(s32[8,6]{1,0:T(8,128)} %param.6) | copy-start | bytes 580
  10.3 42.5 %copy-start.6 = (s32[8]{0:T(128)S(1)}, s32[8]{0:T(128)}, u32[]{:S(2)}) copy-start(s32[8]{0:T(128)} %param.7) | copy-start | bytes 100
  10.3 31.3 %collective-permute-start = (bf16[1,1,6,7,128,128]{4,5,2,3,1,0:T(8,128)(2,1)S(1)}, bf16[1,1,6,7,128,128]{4,5,2,3,1,0:T(8,128)(2,1)S(1)}, u32[]{:S(2)}, u32[]{:S(2)}) collective-permute-start(bf16[1,1,6,7,128,128]{4,5,2,3,1,0:T(8,128)(2,1)S(1)} %maximum_bitcast_fusion), channel_id=1, source_target_pairs={{4,0},{8,4},{12,8},{16,12},{20,16},{24,20},{28,24},{5,1},{9,5},{13... | collective-permute-start | bytes 4128776 | tf_op jit(solution)/shard_map/ppermute | solution.py:20
  13.1 31.6 %collective-permute-start.1 = (bf16[1,1,6,7,128,128]{4,5,2,3,1,0:T(8,128)(2,1)S(1)}, bf16[1,1,6,7,128,128]{4,5,2,3,1,0:T(8,128)(2,1)S(1)}, u32[]{:S(2)}, u32[]{:S(2)}) collective-permute-start(bf16[1,1,6,7,128,128]{4,5,2,3,1,0:T(8,128)(2,1)S(1)} %maximum_bitcast_fusion), channel_id=1, source_target_pairs={{0,4},{4,8},{8,12},{12,16},{16,20},{20,24},{24,28},{1,5},{5,9},{9,... | collective-permute-start | bytes 4128776 | tf_op jit(solution)/shard_map/ppermute | solution.py:19
  41.6 5.2 %copy-start.3 = (bf16[1,1,6,7,128,128]{4,5,2,3,1,0:T(8,128)(2,1)}, bf16[1,1,6,7,128,128]{4,5,2,3,1,0:T(8,128)(2,1)S(1)}, u32[]{:S(2)}) copy-start(bf16[1,1,6,7,128,128]{4,5,2,3,1,0:T(8,128)(2,1)S(1)} %collective-permute-done) | copy-start | bytes 4128772
  46.8 90.3 %collective-permute-start.2 = (bf16[3,1,6,7,128,128]{4,5,2,3,1,0:T(8,128)(2,1)}, bf16[3,1,6,7,128,128]{4,5,2,3,1,0:T(8,128)(2,1)}, u32[]{:S(2)}, u32[]{:S(2)}) collective-permute-start(bf16[3,1,6,7,128,128]{4,5,2,3,1,0:T(8,128)(2,1)} %pad_maximum_fusion), channel_id=1, source_target_pairs={{1,0},{2,1},{3,2},{5,4},{6,5},{7,6},{9,8},{10,9},{11,10},{13,12},{... | collective-permute-start | bytes 12386312 | tf_op jit(solution)/shard_map/ppermute | solution.py:20
  51.2 92.1 %collective-permute-start.3 = (bf16[3,1,6,7,128,128]{4,5,2,3,1,0:T(8,128)(2,1)}, bf16[3,1,6,7,128,128]{4,5,2,3,1,0:T(8,128)(2,1)}, u32[]{:S(2)}, u32[]{:S(2)}) collective-permute-start(bf16[3,1,6,7,128,128]{4,5,2,3,1,0:T(8,128)(2,1)} %pad_maximum_fusion), channel_id=1, source_target_pairs={{0,1},{1,2},{2,3},{4,5},{5,6},{6,7},{8,9},{9,10},{10,11},{12,13},{... | collective-permute-start | bytes 12386312 | tf_op jit(solution)/shard_map/ppermute | solution.py:19
  147.9 4.3 %copy-start.4 = (bf16[6,6,128,128]{3,2,1,0:T(8,128)(2,1)S(1)}, bf16[6,6,128,128]{3,2,1,0:T(8,128)(2,1)}, u32[]{:S(2)}) copy-start(bf16[6,6,128,128]{3,2,1,0:T(8,128)(2,1)} %get-tuple-element.13) | copy-start | bytes 3538948
  152.2 2.0 %copy-start.1 = (bf16[36,2,128,128]{2,3,1,0:T(8,128)(2,1)S(1)}, bf16[36,2,128,128]{2,3,1,0:T(8,128)(2,1)}, u32[]{:S(2)}) copy-start(bf16[36,2,128,128]{2,3,1,0:T(8,128)(2,1)} %gather_fusion) | copy-start | bytes 7077892
where the time goes:
time: 168 us
  waiting for transfers between devices  116 us (69%)
  matrix products  17.1 us (10%)
  other arithmetic  12.1 us (7%)
  local copies, waits for them, and re-layouts  11 us (7%)
  starting transfers between devices  10.5 us (6%)
    ppermute x2, waiting for transfers between devices, padded(): after = lax.ppermute(initial, axis, down)  108 us
    ppermute x2, waiting for transfers between devices, padded(): before = lax.ppermute(last, axis, up)  7.67 us
    ppermute x2, starting transfers between devices, padded(): after = lax.ppermute(initial, axis, down)  7.11 us
    dot_general x8, matrix products, approx_inverse(): jnp.einsum('nij,njk->nik', matrix, iterate, precision=lax.Precision.HIGHEST)  7.06 us
    dot_general x8, matrix products, approx_inverse(): jnp.einsum('nij,njk->nik', iterate, product, precision=lax.Precision.HIGH...  5.47 us
    gather x1, local copies, waits for them, and re-layouts, shards(): picked = table[jnp.arange(slot_count)[None, :], local_rows]  4.3 us
    unnamed x5, other arithmetic  3.96 us
    ppermute x2, starting transfers between devices, padded(): before = lax.ppermute(last, axis, up)  3.38 us
  transfers between devices with their start and end apart: 4, of which 4 were waited for; matrix products, arithmetic and copies ran while one was open for 3% of the time, Pallas kernels for 0%

commit v1 on v0

v1 whole, which is shorter than its diff:
```python
import functools
import jax
import jax.numpy as jnp
from jax import lax
from jax.experimental import pallas as pl
from jax.experimental.pallas import tpu as pltpu
from jax.sharding import PartitionSpec as P

NS_STEPS = 4
MIRROR = (1, 0, 3, 2, 5, 4)
VMEM_LIMIT = 40 * 1024 * 1024
REMOTE = 4
PAIRS = (("col", 1), ("col", 0), ("row", 1), ("row", 0))


def pair_list(size, odd):
    lower = [(i, i + 1) for i in range(odd, size - 1, 2)]
    return lower + [(j, i) for i, j in lower]


def dot(a, b):
    return jnp.dot(a, b, preferred_element_type=jnp.float32)


def dot_t(a, b):
    return lax.dot_general(a, b, (((1,), (1,)), ((), ())), preferred_element_type=jnp.float32)


def halves(value):
    high = value.astype(jnp.bfloat16)
    low = (value - high.astype(jnp.float32)).astype(jnp.bfloat16)
    return high, low


def approx_inverses(matrices, exact):
    size = matrices[0].shape[0]
    eye = (
        lax.broadcasted_iota(jnp.int32, (size, size), 0)
        == lax.broadcasted_iota(jnp.int32, (size, size), 1)
    ).astype(jnp.float32)
    iterates, residuals = [], []
    for matrix in matrices:
        turned = matrix.T
        column = jnp.max(jnp.sum(jnp.abs(matrix), axis=0, keepdims=True), axis=1, keepdims=True)
        row = jnp.max(jnp.sum(jnp.abs(turned), axis=0, keepdims=True), axis=1, keepdims=True)
        scale = 1.0 / (column * row)
        if exact:
            square = dot_t(matrix.astype(jnp.bfloat16), matrix.astype(jnp.bfloat16))
        else:
            high, low = halves(matrix)
            left = jnp.concatenate([high, low], axis=1)
            right = jnp.concatenate(
                [
                    jnp.concatenate([high, high], axis=1),
                    jnp.concatenate([low, low], axis=1),
                ],
                axis=0,
            )
            both = dot_t(left, right)
            square = both[:, :size] + both[:, size:]
        iterates.append(turned * scale)
        residuals.append(eye - square * scale)
    for step in range(NS_STEPS):
        last = step == NS_STEPS - 1
        for n in range(len(matrices)):
            r_high, r_low = halves(residuals[n])
            x_high, x_low = halves(iterates[n])
            row = jnp.concatenate([r_high, r_low], axis=1)
            right = jnp.concatenate([row, row], axis=0)
            left = jnp.concatenate([x_high, x_low], axis=1)
            if not last:
                left = jnp.concatenate([left, row], axis=0)
            both = dot(left, right)
            both = both[:, :size] + both[:, size:]
            iterates[n] = iterates[n] + both[:size]
            if not last:
                residuals[n] = both[size:]
    return iterates


def slot_order():
    row = lax.axis_index("row") % 2
    col = lax.axis_index("col") % 2
    return (3 - col, 2 + col, 1 - row, row)


def first_kernel(capacity, diag_hbm, off_hbm, *rest):
    payloads, (inverse, diag, off, sems) = rest[:REMOTE], rest[REMOTE:]
    slots = slot_order()
    copy_diag = pltpu.make_async_copy(diag_hbm.at[pl.ds(0, capacity)], diag, sems.at[0])
    copy_off = pltpu.make_async_copy(off_hbm.at[pl.ds(0, capacity), pl.ds(0, REMOTE)], off, sems.at[1])
    copy_diag.start()
    copy_off.start()
    copy_diag.wait()
    inverses = approx_inverses([diag[n].astype(jnp.float32) for n in range(capacity)], True)
    inverses = [value.astype(jnp.bfloat16) for value in inverses]
    copy_off.wait()
    for n in range(capacity):
        inverse[n] = inverses[n]
        for j in range(0, REMOTE, 2):
            scaled = dot(inverses[n], jnp.concatenate([off[n, slots[j]], off[n, slots[j + 1]]], axis=1))
            for i in range(2):
                payloads[j + i][n] = inverses[n]
                payloads[j + i][capacity + n] = scaled[:, i * 128 : (i + 1) * 128].astype(jnp.bfloat16)


def local_kernel(
    capacity, rows, neighbors, levels, off_hbm, inverse, p0, p1, p2, p3,
    factor_hbm, schur, lower, scaled, off, nothing, sems,
):
    payloads = (p0, p1, p2, p3)
    slots = slot_order()
    start = rows - capacity
    copy_off = pltpu.make_async_copy(off_hbm.at[:, pl.ds(REMOTE, 2)], off, sems.at[0])
    copy_off.start()
    nothing[...] = jnp.zeros_like(nothing)

    def each_remote(act):
        for n in range(capacity):

            @pl.when(levels[n] == 0)
            def _():
                for j in range(REMOTE):
                    target = factor_hbm.at[n, slots[j]]

                    @pl.when(neighbors[n, slots[j]] >= 0)
                    def _():
                        act(pltpu.make_async_copy(payloads[j].at[capacity + n], target, sems.at[1]))

                    @pl.when(neighbors[n, slots[j]] < 0)
                    def _():
                        act(pltpu.make_async_copy(nothing, target, sems.at[1]))

    each_remote(lambda c: c.start())
    copy_off.wait()
    for n in range(capacity):
        both = dot(inverse[n], jnp.concatenate([off[n, 0], off[n, 1]], axis=1))
        for i in range(2):
            part = both[:, i * 128 : (i + 1) * 128]
            part = jnp.where(neighbors[n, REMOTE + i] >= 0, part, 0.0)
            scaled[n, i] = part.astype(jnp.bfloat16)

    def local_row(t, carry):
        q = start + t
        total = None
        for i in range(2):
            named = neighbors[q, REMOTE + i]
            place = jnp.clip(named % rows, 0, capacity - 1)
            block = jnp.where(named >= 0, off[q, i].astype(jnp.float32), 0.0).astype(jnp.bfloat16)
            both = dot(block, jnp.concatenate([inverse[place], scaled[place, 1 - i]], axis=1))
            lower[t, i] = both[:, :128].astype(jnp.bfloat16)
            total = both[:, 128:] if total is None else total + both[:, 128:]
        schur[t] = total
        return carry

    lax.fori_loop(0, capacity, local_row, 0)

    def each_local(act):
        for n in range(rows):
            target = factor_hbm.at[n, pl.ds(REMOTE, 2)]
            if n < capacity:

                @pl.when(levels[n] == 0)
                def _():
                    act(pltpu.make_async_copy(scaled.at[n], target, sems.at[2]))

            if n >= start:

                @pl.when(levels[n] == 1)
                def _():
                    act(pltpu.make_async_copy(lower.at[n - start], target, sems.at[2]))

    each_local(lambda c: c.start())
    each_remote(lambda c: c.wait())
    each_local(lambda c: c.wait())


def second_kernel(
    capacity, rows, neighbors, levels, diag_hbm, off_hbm, factor_in, inverse, r0, r1, r2, r3, schur,
    pivot, factor_hbm, diag, off, lower, sems,
):
    del factor_in
    received = (r0, r1, r2, r3)
    slots = slot_order()
    start = rows - capacity
    copy_diag = pltpu.make_async_copy(diag_hbm.at[pl.ds(start, capacity)], diag, sems.at[0])
    copy_off = pltpu.make_async_copy(off_hbm.at[pl.ds(start, capacity), pl.ds(0, REMOTE)], off, sems.at[1])
    copy_diag.start()
    copy_off.start()
    copy_diag.wait()
    copy_off.wait()
    pivots = []
    for t in range(capacity):
        q = start + t
        total = schur[t]
        for j in range(REMOTE):
            slot = slots[j]
            named = neighbors[q, slot]
            place = jnp.clip(named % rows, 0, capacity - 1)
            block = jnp.where(named >= 0, off[t, slot].astype(jnp.float32), 0.0).astype(jnp.bfloat16)
            both = dot(block, jnp.concatenate([received[j][place], received[j][capacity + place]], axis=1))
            lower[t, slot] = both[:, :128].astype(jnp.bfloat16)
            total = total + both[:, 128:]
        pivots.append(diag[t].astype(jnp.float32) - total)

    def each_lower(act):
        for t in range(capacity):

            @pl.when(levels[start + t] == 1)
            def _():
                act(pltpu.make_async_copy(lower.at[t], factor_hbm.at[start + t, pl.ds(0, REMOTE)], sems.at[2]))

    each_lower(lambda c: c.start())
    inverses = approx_inverses(pivots, False)
    for n in range(rows):
        if n < start:
            pivot[n] = inverse[n]
        elif n >= capacity:
            pivot[n] = inverses[n - start].astype(jnp.bfloat16)
        else:
            pivot[n] = jnp.where(
                levels[n] == 0, inverse[n].astype(jnp.float32), inverses[n - start]
            ).astype(jnp.bfloat16)
    each_lower(lambda c: c.wait())


def shards(diag_blocks, off_blocks, neighbors, levels):
    rows, slots = off_blocks.shape[:2]
    size = diag_blocks.shape[1]
    capacity = 3 * rows // 4
    smem = pl.BlockSpec(memory_space=pltpu.SMEM)
    vmem = pl.BlockSpec(memory_space=pltpu.VMEM)
    hbm = pl.BlockSpec(memory_space=pltpu.HBM)
    params = pltpu.CompilerParams(vmem_limit_bytes=VMEM_LIMIT)
    bf16 = jnp.bfloat16
    payload = jax.ShapeDtypeStruct((2 * capacity, size, size), bf16)

    diag_blocks = pltpu.with_memory_space_constraint(diag_blocks, pltpu.HBM)
    off_blocks = pltpu.with_memory_space_constraint(off_blocks, pltpu.HBM)
    *payloads, inverse = pl.pallas_call(
        functools.partial(first_kernel, capacity),
        out_shape=[payload] * REMOTE + [jax.ShapeDtypeStruct((capacity, size, size), bf16)],
        in_specs=[hbm, hbm],
        out_specs=[vmem] * (REMOTE + 1),
        scratch_shapes=[
            pltpu.VMEM((capacity, size, size), bf16),
            pltpu.VMEM((capacity, REMOTE, size, size), bf16),
            pltpu.SemaphoreType.DMA((2,)),
        ],
        compiler_params=params,
        name="first_inverses",
    )(diag_blocks, off_blocks)

    received = []
    for j, (axis, odd) in enumerate(PAIRS):
        received.append(lax.ppermute(payloads[j], axis, pair_list(lax.axis_size(axis), odd)))

    factor, schur = pl.pallas_call(
        functools.partial(local_kernel, capacity, rows),
        out_shape=[
            jax.ShapeDtypeStruct((rows, slots, size, size), bf16),
            jax.ShapeDtypeStruct((capacity, size, size), jnp.float32),
        ],
        in_specs=[smem, smem, hbm] + [vmem] * (REMOTE + 1),
        out_specs=[hbm, vmem],
        scratch_shapes=[
            pltpu.VMEM((capacity, 2, size, size), bf16),
            pltpu.VMEM((capacity, 2, size, size), bf16),
            pltpu.VMEM((rows, 2, size, size), bf16),
            pltpu.VMEM((size, size), bf16),
            pltpu.SemaphoreType.DMA((3,)),
        ],
        compiler_params=params,
        cost_estimate=pl.CostEstimate(flops=400_000_000, bytes_accessed=4_000_000, transcendentals=0),
        name="local_slots",
    )(neighbors, levels, off_blocks, inverse, *payloads)

    pivot, factor = pl.pallas_call(
        functools.partial(second_kernel, capacity, rows),
        out_shape=[
            jax.ShapeDtypeStruct((rows, size, size), bf16),
            jax.ShapeDtypeStruct((rows, slots, size, size), bf16),
        ],
        in_specs=[smem, smem, hbm, hbm, hbm] + [vmem] * (REMOTE + 2),
        out_specs=[vmem, hbm],
        scratch_shapes=[
            pltpu.VMEM((capacity, size, size), bf16),
            pltpu.VMEM((capacity, REMOTE, size, size), bf16),
            pltpu.VMEM((capacity, REMOTE, size, size), bf16),
            pltpu.SemaphoreType.DMA((3,)),
        ],
        input_output_aliases={4: 1},
        compiler_params=params,
        name="second_inverses",
    )(neighbors, levels, diag_blocks, off_blocks, factor, inverse, *received, schur)
    return (pivot, factor)


def solution(mesh):
    in_specs = (
        P(("row", "col"), None, None),
        P(("row", "col"), None, None, None),
        P(("row", "col"), None),
        P(("row", "col")),
    )
    out_specs = (P(("row", "col"), None, None), P(("row", "col"), None, None, None))
    return jax.shard_map(shards, mesh=mesh, in_specs=in_specs, out_specs=out_specs, check_vma=False)
```

time: 168 us -> 27.1 us (0.16)
  the two profiles are of different devices: /device:TPU:28 before, /device:TPU:1 now
where the time goes in v1:
time: 27.1 us; the launch traced here: 26.8 us
  Pallas kernels  11.8 us (44%)
  starting transfers between devices  9.69 us (36%)
  waiting for transfers between devices  4.65 us (17%)
  between operations  0.71 us (3%)
    ppermute x4, starting transfers between devices, shards(): lax.ppermute(payloads[j], axis, pair_list(lax.axis_size(axis), odd))  9.69 us
    pallas_call x1, Pallas kernels, shards(): pl.pallas_call(functools.partial(second_kernel, capacity, rows), out_shap...  4.95 us
    ppermute x4, waiting for transfers between devices, shards(): lax.ppermute(payloads[j], axis, pair_list(lax.axis_size(axis), odd))  4.65 us
    pallas_call x1, Pallas kernels, shards(): pl.pallas_call(functools.partial(local_kernel, capacity, rows), out_shape...  4.01 us
    pallas_call x1, Pallas kernels, shards(): pl.pallas_call(functools.partial(first_kernel, capacity), out_shape=[payl...  2.81 us
  transfers between devices with their start and end apart: 4, of which 2 were waited for; matrix products, arithmetic and copies ran while one was open for 0% of the time, Pallas kernels for 15%

profile of v1, /device:TPU:1, one launch (start us, length us, event | category | flops | bytes accessed | tf_op | source)
XLA Modules:
  0.0 26.8 jit_solution(3929387517058189112)
XLA Ops:
  0.6 0.0 copy-start.1
  0.6 0.0 copy-start
  0.6 2.8 %first_inverses.1 = (bf16[12,128,128]{2,1,0:T(8,128)(2,1)S(1)}, bf16[12,128,128]{2,1,0:T(8,128)(2,1)S(1)}, bf16[12,128,128]{2,1,0:T(8,128)(2,1)S(1)}, bf16[12,12...) custom-call(bf16[8,128,128]{2,1,0:T(8,128)(2,1)} %diag_hbm.3, bf16[8,6,128,128]{3,2,1,0:T(8,128)(2,1)} %off_hbm.5), custom_call_target="tpu_custom_call" | custom-call | tf_op jit(solution)/shard_map/first_inverses/pallas_call | solution.py:240
  3.5 0.7 %collective-permute-start = (bf16[12,128,128]{2,1,0:T(8,128)(2,1)S(1)}, bf16[12,128,128]{2,1,0:T(8,128)(2,1)S(1)}, u32[]{:S(2)}, u32[]{:S(2)}) collective-permute-start(bf16[12,128,128]{2,1,0:T(8,128)(2,1)S(1)} %get-tuple-element.10.p0), channel_id=1, source_target_pairs={{1,2},{2,1},{5,6},{6,5},{9,10},{10,9},{13,14},{14,13},{17,18},{18,... | collective-permute-start | bytes 1179656 | tf_op jit(solution)/shard_map/ppermute | solution.py:256
  4.2 4.7 %collective-permute-start.1 = (bf16[12,128,128]{2,1,0:T(8,128)(2,1)S(1)}, bf16[12,128,128]{2,1,0:T(8,128)(2,1)S(1)}, u32[]{:S(2)}, u32[]{:S(2)}) collective-permute-start(bf16[12,128,128]{2,1,0:T(8,128)(2,1)S(1)} %get-tuple-element.11.p1), channel_id=1, source_target_pairs={{0,1},{2,3},{1,0},{3,2},{4,5},{6,7},{5,4},{7,6},{8,9},{10,11},{9,8... | collective-permute-start | bytes 1179656 | tf_op jit(solution)/shard_map/ppermute | solution.py:256
  8.9 4.2 %collective-permute-start.2 = (bf16[12,128,128]{2,1,0:T(8,128)(2,1)S(1)}, bf16[12,128,128]{2,1,0:T(8,128)(2,1)S(1)}, u32[]{:S(2)}, u32[]{:S(2)}) collective-permute-start(bf16[12,128,128]{2,1,0:T(8,128)(2,1)S(1)} %get-tuple-element.12.p2), channel_id=1, source_target_pairs={{4,8},{12,16},{20,24},{8,4},{16,12},{24,20},{5,9},{13,17},{21,25},... | collective-permute-start | bytes 1179656 | tf_op jit(solution)/shard_map/ppermute | solution.py:256
  13.1 0.1 collective-permute-start.3
  13.2 0.0 copy-done.1
  13.2 0.0 copy-done
  13.2 4.0 %local_slots.1 = (bf16[8,6,128,128]{3,2,1,0:T(8,128)(2,1)}, f32[6,128,128]{2,1,0:T(8,128)S(1)}) custom-call(s32[8,6]{1,0:T(8,128)S(1)} %copy-done, s32[8]{0:T(128)S(1)} %copy-done.1, bf16[8,6,128,128]{3,2,1,0:T(8,128)(2,1)} %off_hbm.5, bf16[6,128,128]{2,1,0:T(8,128)(2,1)S(1)} %get-tuple-element.9.inverse, bf16[12,128,128]{2,1,0:T(8,128)(2,1)S(1)} %get-tuple-element.10.p0, ...), custom_call_target="tpu_custom_call" | custom-call | flops 400000000 | bytes 4000000 | tf_op jit(solution)/shard_map/local_slots/pallas_call | solution.py:258
  17.2 0.0 collective-permute-done.r0
  17.2 0.2 collective-permute-done.1.r1
  17.4 4.5 %collective-permute-done.2.r2 = bf16[12,128,128]{2,1,0:T(8,128)(2,1)S(1)} collective-permute-done((bf16[12,128,128]{2,1,0:T(8,128)(2,1)S(1)}, bf16[12,128,128]{2,1,0:T(8,128)(2,1)S(1)}, u32[]{:S(2)}, u32[]{:S(2)}) %collective-permute-start.2) | collective-permute-done | bytes 393248 | tf_op jit(solution)/shard_map/ppermute | solution.py:256
  21.9 0.0 collective-permute-done.3.r3
  21.9 5.0 %second_inverses.1 = (bf16[8,128,128]{2,1,0:T(8,128)(2,1)}, bf16[8,6,128,128]{3,2,1,0:T(8,128)(2,1)}) custom-call(s32[8,6]{1,0:T(8,128)S(1)} %copy-done, s32[8]{0:T(128)S(1)} %copy-done.1, bf16[8,128,128]{2,1,0:T(8,128)(2,1)} %diag_hbm.3, bf16[8,6,128,128]{3,2,1,0:T(8,128)(2,1)} %off_hbm.5, ...), custom_call_target="tpu_custom_call", output_to_operand_aliasing={{1}: (4, {})} | custom-call | tf_op jit(solution)/shard_map/second_inverses/pallas_call | solution.py:278
Async XLA Ops:
  0.6 12.6 %copy-start.1 = (s32[8]{0:T(128)S(1)}, s32[8]{0:T(128)}, u32[]{:S(2)}) copy-start(s32[8]{0:T(128)} %levels.3) | copy-start | bytes 100
  0.6 12.6 %copy-start = (s32[8,6]{1,0:T(8,128)S(1)}, s32[8,6]{1,0:T(8,128)}, u32[]{:S(2)}) copy-start(s32[8,6]{1,0:T(8,128)} %neighbors.3) | copy-start | bytes 580
  3.5 13.8 %collective-permute-start = (bf16[12,128,128]{2,1,0:T(8,128)(2,1)S(1)}, bf16[12,128,128]{2,1,0:T(8,128)(2,1)S(1)}, u32[]{:S(2)}, u32[]{:S(2)}) collective-permute-start(bf16[12,128,128]{2,1,0:T(8,128)(2,1)S(1)} %get-tuple-element.10.p0), channel_id=1, source_target_pairs={{1,2},{2,1},{5,6},{6,5},{9,10},{10,9},{13,14},{14,13},{17,18},{18,... | collective-permute-start | bytes 1179656 | tf_op jit(solution)/shard_map/ppermute | solution.py:256
  4.2 13.2 %collective-permute-start.1 = (bf16[12,128,128]{2,1,0:T(8,128)(2,1)S(1)}, bf16[12,128,128]{2,1,0:T(8,128)(2,1)S(1)}, u32[]{:S(2)}, u32[]{:S(2)}) collective-permute-start(bf16[12,128,128]{2,1,0:T(8,128)(2,1)S(1)} %get-tuple-element.11.p1), channel_id=1, source_target_pairs={{0,1},{2,3},{1,0},{3,2},{4,5},{6,7},{5,4},{7,6},{8,9},{10,11},{9,8... | collective-permute-start | bytes 1179656 | tf_op jit(solution)/shard_map/ppermute | solution.py:256
  8.9 13.0 %collective-permute-start.2 = (bf16[12,128,128]{2,1,0:T(8,128)(2,1)S(1)}, bf16[12,128,128]{2,1,0:T(8,128)(2,1)S(1)}, u32[]{:S(2)}, u32[]{:S(2)}) collective-permute-start(bf16[12,128,128]{2,1,0:T(8,128)(2,1)S(1)} %get-tuple-element.12.p2), channel_id=1, source_target_pairs={{4,8},{12,16},{20,24},{8,4},{16,12},{24,20},{5,9},{13,17},{21,25},... | collective-permute-start | bytes 1179656 | tf_op jit(solution)/shard_map/ppermute | solution.py:256
  13.1 8.8 %collective-permute-start.3 = (bf16[12,128,128]{2,1,0:T(8,128)(2,1)S(1)}, bf16[12,128,128]{2,1,0:T(8,128)(2,1)S(1)}, u32[]{:S(2)}, u32[]{:S(2)}) collective-permute-start(bf16[12,128,128]{2,1,0:T(8,128)(2,1)S(1)} %get-tuple-element.13.p3), channel_id=1, source_target_pairs={{0,4},{8,12},{16,20},{24,28},{4,0},{12,8},{20,16},{28,24},{1,5},{9... | collective-permute-start | bytes 1179656 | tf_op jit(solution)/shard_map/ppermute | solution.py:256

commit v2 on v1

v2 whole, which is shorter than its diff:
```python
import functools
import jax
import jax.numpy as jnp
from jax import lax
from jax.experimental import pallas as pl
from jax.experimental.pallas import tpu as pltpu
from jax.sharding import PartitionSpec as P

NS_STEPS = 4
MIRROR = (1, 0, 3, 2, 5, 4)
VMEM_LIMIT = 40 * 1024 * 1024
REMOTE = 4


def dot(a, b):
    return jnp.dot(a, b, preferred_element_type=jnp.float32)


def dot_t(a, b):
    return lax.dot_general(a, b, (((1,), (1,)), ((), ())), preferred_element_type=jnp.float32)


def halves(value):
    high = value.astype(jnp.bfloat16)
    low = (value - high.astype(jnp.float32)).astype(jnp.bfloat16)
    return high, low


def approx_inverses(matrices, exact):
    size = matrices[0].shape[0]
    eye = (
        lax.broadcasted_iota(jnp.int32, (size, size), 0)
        == lax.broadcasted_iota(jnp.int32, (size, size), 1)
    ).astype(jnp.float32)
    iterates, residuals = [], []
    for matrix in matrices:
        turned = matrix.T
        column = jnp.max(jnp.sum(jnp.abs(matrix), axis=0, keepdims=True), axis=1, keepdims=True)
        row = jnp.max(jnp.sum(jnp.abs(turned), axis=0, keepdims=True), axis=1, keepdims=True)
        scale = 1.0 / (column * row)
        if exact:
            square = dot_t(matrix.astype(jnp.bfloat16), matrix.astype(jnp.bfloat16))
        else:
            high, low = halves(matrix)
            left = jnp.concatenate([high, low], axis=1)
            right = jnp.concatenate(
                [
                    jnp.concatenate([high, high], axis=1),
                    jnp.concatenate([low, low], axis=1),
                ],
                axis=0,
            )
            both = dot_t(left, right)
            square = both[:, :size] + both[:, size:]
        iterates.append(turned * scale)
        residuals.append(eye - square * scale)
    for step in range(NS_STEPS):
        last = step == NS_STEPS - 1
        for n in range(len(matrices)):
            r_high, r_low = halves(residuals[n])
            x_high, x_low = halves(iterates[n])
            row = jnp.concatenate([r_high, r_low], axis=1)
            right = jnp.concatenate([row, row], axis=0)
            left = jnp.concatenate([x_high, x_low], axis=1)
            if not last:
                left = jnp.concatenate([left, row], axis=0)
            both = dot(left, right)
            both = both[:, :size] + both[:, size:]
            iterates[n] = iterates[n] + both[:size]
            if not last:
                residuals[n] = both[size:]
    return iterates


def slot_order():
    row = lax.axis_index("row") % 2
    across = 1 - row
    return (row, 2 + row, across, 3 - row), (row, 3 - row, across, 2 + row)


def transfers(rows, cols):
    steps = [[], [], [], []]
    for r in range(rows):
        for c in range(cols):
            here = r * cols + c
            up, down = (1, 3) if r % 2 == 0 else (3, 1)
            if c + 1 < cols:
                steps[up].append((here, here + 1))
            if c > 0:
                steps[down].append((here, here - 1))
            if r + 1 < rows:
                pair = [(here, here + cols), (here + cols, here)]
                steps[0 if r % 2 == 0 else 2].extend(pair)
    return steps


def masked(block, named):
    return jnp.where(named >= 0, block, jnp.zeros_like(block))


def first_kernel(capacity, diag_hbm, off_hbm, *rest):
    payloads, (inverse, diag, off, sems) = rest[:REMOTE], rest[REMOTE:]
    slots, _ = slot_order()
    copy_diag = pltpu.make_async_copy(diag_hbm, diag, sems.at[0])
    copy_off = pltpu.make_async_copy(off_hbm, off, sems.at[1])
    copy_diag.start()
    copy_off.start()
    copy_diag.wait()
    inverses = approx_inverses([diag[n].astype(jnp.float32) for n in range(capacity)], True)
    inverses = [value.astype(jnp.bfloat16) for value in inverses]
    copy_off.wait()
    for n in range(capacity):
        inverse[n] = inverses[n]
        for j in range(0, REMOTE, 2):
            scaled = dot(inverses[n], jnp.concatenate([off[n, slots[j]], off[n, slots[j + 1]]], axis=1))
            for i in range(2):
                payloads[j + i][n] = inverses[n]
                payloads[j + i][capacity + n] = scaled[:, i * 128 : (i + 1) * 128].astype(jnp.bfloat16)


def local_kernel(
    capacity, rows, neighbors, levels, diag, off, inverse, p0, p1, p2, p3,
    factor_hbm, base, lower, scaled, nothing, sems,
):
    payloads = (p0, p1, p2, p3)
    slots, _ = slot_order()
    start = rows - capacity
    nothing[...] = jnp.zeros_like(nothing)

    def each_remote(act):
        for n in range(capacity):

            @pl.when(levels[n] == 0)
            def _():
                for j in range(REMOTE):
                    target = factor_hbm.at[n, slots[j]]

                    @pl.when(neighbors[n, slots[j]] >= 0)
                    def _():
                        act(pltpu.make_async_copy(payloads[j].at[capacity + n], target, sems.at[0]))

                    @pl.when(neighbors[n, slots[j]] < 0)
                    def _():
                        act(pltpu.make_async_copy(nothing, target, sems.at[0]))

    each_remote(lambda c: c.start())
    for n in range(capacity):
        both = dot(inverse[n], jnp.concatenate([off[n, REMOTE], off[n, REMOTE + 1]], axis=1))
        for i in range(2):
            part = both[:, i * 128 : (i + 1) * 128]
            scaled[n, i] = masked(part, neighbors[n, REMOTE + i]).astype(jnp.bfloat16)

    def local_row(t, carry):
        q = start + t
        total = diag[q].astype(jnp.float32)
        for i in range(2):
            named = neighbors[q, REMOTE + i]
            place = jnp.clip(named % rows, 0, capacity - 1)
            block = masked(off[q, REMOTE + i], named)
            both = dot(block, jnp.concatenate([inverse[place], scaled[place, 1 - i]], axis=1))
            lower[t, i] = both[:, :128].astype(jnp.bfloat16)
            total = total - both[:, 128:]
        base[t] = total
        return carry

    lax.fori_loop(0, capacity, local_row, 0)

    def each_local(act):
        for n in range(rows):
            target = factor_hbm.at[n, pl.ds(REMOTE, 2)]
            if n < capacity:

                @pl.when(levels[n] == 0)
                def _():
                    act(pltpu.make_async_copy(scaled.at[n], target, sems.at[1]))

            if n >= start:

                @pl.when(levels[n] == 1)
                def _():
                    act(pltpu.make_async_copy(lower.at[n - start], target, sems.at[1]))

    each_local(lambda c: c.start())
    each_remote(lambda c: c.wait())
    each_local(lambda c: c.wait())


def take(capacity, rows, t, arrived, neighbors, off, received, lower, total):
    _, slots = slot_order()
    q = rows - capacity + t
    for i, j in enumerate(arrived):
        named = neighbors[q, slots[j]]
        place = jnp.clip(named % rows, 0, capacity - 1)
        block = masked(off[q, slots[j]], named)
        both = dot(block, jnp.concatenate([received[i][place], received[i][capacity + place]], axis=1))
        lower[t, i] = both[:, :128].astype(jnp.bfloat16)
        total = total - both[:, 128:]
    return total


def early_kernel(capacity, rows, arrived, neighbors, off, base, ra, rb, total, lower):
    for t in range(capacity):
        total[t] = take(capacity, rows, t, arrived, neighbors, off, (ra, rb), lower, base[t])


def second_kernel(
    capacity, rows, before, arrived, neighbors, levels, factor_in, off, inverse, total, lower_before, ra, rb,
    pivot, factor_hbm, lower, sems,
):
    del factor_in
    _, slots = slot_order()
    start = rows - capacity

    def each_lower(source, which, sem, act):
        for t in range(capacity):

            @pl.when(levels[start + t] == 1)
            def _():
                for i, j in enumerate(which):
                    act(pltpu.make_async_copy(source.at[t, i], factor_hbm.at[start + t, slots[j]], sem))

    each_lower(lower_before, before, sems.at[0], lambda c: c.start())
    pivots = [
        take(capacity, rows, t, arrived, neighbors, off, (ra, rb), lower, total[t]) for t in range(capacity)
    ]
    each_lower(lower, arrived, sems.at[1], lambda c: c.start())
    inverses = approx_inverses(pivots, False)
    for n in range(rows):
        if n < start:
            pivot[n] = inverse[n]
        elif n >= capacity:
            pivot[n] = inverses[n - start].astype(jnp.bfloat16)
        else:
            pivot[n] = jnp.where(levels[n] == 0, inverse[n], inverses[n - start].astype(jnp.bfloat16))
    each_lower(lower_before, before, sems.at[0], lambda c: c.wait())
    each_lower(lower, arrived, sems.at[1], lambda c: c.wait())


def shards(diag_blocks, off_blocks, neighbors, levels):
    rows, slots = off_blocks.shape[:2]
    size = diag_blocks.shape[1]
    capacity = 3 * rows // 4
    smem = pl.BlockSpec(memory_space=pltpu.SMEM)
    vmem = pl.BlockSpec(memory_space=pltpu.VMEM)
    hbm = pl.BlockSpec(memory_space=pltpu.HBM)
    params = pltpu.CompilerParams(vmem_limit_bytes=VMEM_LIMIT)
    bf16 = jnp.bfloat16
    payload = jax.ShapeDtypeStruct((2 * capacity, size, size), bf16)
    totals = jax.ShapeDtypeStruct((capacity, size, size), jnp.float32)
    factors = jax.ShapeDtypeStruct(off_blocks.shape, bf16)

    diag_blocks = pltpu.with_memory_space_constraint(diag_blocks, pltpu.HBM)
    off_blocks = pltpu.with_memory_space_constraint(off_blocks, pltpu.HBM)
    *payloads, inverse, diag, off = pl.pallas_call(
        functools.partial(first_kernel, capacity),
        out_shape=[payload] * REMOTE
        + [
            jax.ShapeDtypeStruct((capacity, size, size), bf16),
            jax.ShapeDtypeStruct((rows, size, size), bf16),
            factors,
        ],
        in_specs=[hbm, hbm],
        out_specs=[vmem] * (REMOTE + 3),
        scratch_shapes=[pltpu.SemaphoreType.DMA((2,))],
        compiler_params=params,
        name="first_inverses",
    )(diag_blocks, off_blocks)

    steps = transfers(lax.axis_size("row"), lax.axis_size("col"))
    received = [lax.ppermute(payloads[j], ("row", "col"), steps[j]) for j in range(REMOTE)]

    factor, base = pl.pallas_call(
        functools.partial(local_kernel, capacity, rows),
        out_shape=[factors, totals],
        in_specs=[smem, smem] + [vmem] * (REMOTE + 3),
        out_specs=[hbm, vmem],
        scratch_shapes=[
            pltpu.VMEM((capacity, 2, size, size), bf16),
            pltpu.VMEM((capacity, 2, size, size), bf16),
            pltpu.VMEM((size, size), bf16),
            pltpu.SemaphoreType.DMA((2,)),
        ],
        compiler_params=params,
        cost_estimate=pl.CostEstimate(flops=400_000_000, bytes_accessed=4_000_000, transcendentals=0),
        name="local_slots",
    )(neighbors, levels, diag, off, inverse, *payloads)

    before, after = (0, 1), (2, 3)
    total, lower = pl.pallas_call(
        functools.partial(early_kernel, capacity, rows, before),
        out_shape=[totals, jax.ShapeDtypeStruct((capacity, 2, size, size), bf16)],
        in_specs=[smem] + [vmem] * 4,
        out_specs=[vmem, vmem],
        compiler_params=params,
        name="early_slots",
    )(neighbors, off, base, *(received[j] for j in before))

    pivot, factor = pl.pallas_call(
        functools.partial(second_kernel, capacity, rows, before, after),
        out_shape=[jax.ShapeDtypeStruct((rows, size, size), bf16), factors],
        in_specs=[smem, smem, hbm] + [vmem] * 6,
        out_specs=[vmem, hbm],
        scratch_shapes=[
            pltpu.VMEM((capacity, 2, size, size), bf16),
            pltpu.SemaphoreType.DMA((2,)),
        ],
        input_output_aliases={2: 1},
        compiler_params=params,
        name="second_inverses",
    )(neighbors, levels, factor, off, inverse, total, lower, *(received[j] for j in after))
    return (pivot, factor)


def solution(mesh):
    in_specs = (
        P(("row", "col"), None, None),
        P(("row", "col"), None, None, None),
        P(("row", "col"), None),
        P(("row", "col")),
    )
    out_specs = (P(("row", "col"), None, None), P(("row", "col"), None, None, None))
    return jax.shard_map(shards, mesh=mesh, in_specs=in_specs, out_specs=out_specs, check_vma=False)
```

time: 27.1 us -> 24.2 us (0.89)
  waiting for transfers between devices: 4.65 us -> 1.71 us
  starting transfers between devices: 9.69 us -> 11.3 us
  Pallas kernels: 11.8 us -> 10.3 us
    ppermute x4, waiting for transfers between devices: 4.65 us -> 1.71 us  [shards(): lax.ppermute(payloads[j], ('row', 'col'), steps[j])]
    ppermute x4, starting transfers between devices: 9.69 us -> 11.3 us  [shards(): lax.ppermute(payloads[j], ('row', 'col'), steps[j])]
    pallas_call x1, Pallas kernels: 4.01 us -> 2.81 us  [shards(): pl.pallas_call(functools.partial(local_kernel, capacity, rows), out_shape...]
    pallas_call x1 -> x2, Pallas kernels: 4.95 us -> 4.65 us  [the longest x1 3.65 us: shards(): pl.pallas_call(functools.partial(second_kernel, capacity, rows, before, a...]
  transfers between devices with their start and end apart: 4 -> 4, of which waited for: 2 -> 1; matrix products, arithmetic and copies ran while one was open for 0% -> 0% of each run, Pallas kernels for 15% -> 16%
where the time goes in v2:
time: 24.2 us; the launch traced here: 24 us
  starting transfers between devices  11.3 us (47%)
  Pallas kernels  10.3 us (43%)
  waiting for transfers between devices  1.71 us (7%)
  between operations  0.73 us (3%)
    ppermute x4, starting transfers between devices, shards(): lax.ppermute(payloads[j], ('row', 'col'), steps[j])  11.3 us
    pallas_call x1, Pallas kernels, shards(): pl.pallas_call(functools.partial(second_kernel, capacity, rows, before, a...  3.65 us
    pallas_call x1, Pallas kernels, shards(): pl.pallas_call(functools.partial(first_kernel, capacity), out_shape=[payl...  2.84 us
    pallas_call x1, Pallas kernels, shards(): pl.pallas_call(functools.partial(local_kernel, capacity, rows), out_shape...  2.81 us
    ppermute x4, waiting for transfers between devices, shards(): lax.ppermute(payloads[j], ('row', 'col'), steps[j])  1.71 us
    pallas_call x1, Pallas kernels, shards(): pl.pallas_call(functools.partial(early_kernel, capacity, rows, before), o...  0.99 us
  transfers between devices with their start and end apart: 4, of which 1 were waited for; matrix products, arithmetic and copies ran while one was open for 0% of the time, Pallas kernels for 16%

profile of v2, /device:TPU:1, one launch (start us, length us, event | category | flops | bytes accessed | tf_op | source)
XLA Modules:
  0.0 24.0 jit_solution(11524560818316133582)
XLA Ops:
  0.6 0.0 copy-start
  0.6 0.0 copy-start.1
  0.7 2.8 %first_inverses.1 = (bf16[12,128,128]{2,1,0:T(8,128)(2,1)S(1)}, bf16[12,128,128]{2,1,0:T(8,128)(2,1)S(1)}, bf16[12,128,128]{2,1,0:T(8,128)(2,1)S(1)}, bf16[12,12...) custom-call(bf16[8,128,128]{2,1,0:T(8,128)(2,1)} %diag_hbm.1, ...), custom_call_target="tpu_custom_call" | custom-call | tf_op jit(solution)/shard_map/first_inverses/pallas_call | solution.py:254
  3.5 0.1 collective-permute-start
  3.6 1.3 %collective-permute-start.1 = (bf16[12,128,128]{2,1,0:T(8,128)(2,1)S(1)}, bf16[12,128,128]{2,1,0:T(8,128)(2,1)S(1)}, u32[]{:S(2)}, u32[]{:S(2)}) collective-permute-start(bf16[12,128,128]{2,1,0:T(8,128)(2,1)S(1)} %get-tuple-element.17.p1), channel_id=1, source_target_pairs={{0,1},{1,2},{2,3},{5,4},{6,5},{7,6},{8,9},{9,10},{10,11},{13,12},{... | collective-permute-start | bytes 1179656 | tf_op jit(solution)/shard_map/ppermute | solution.py:270
  4.9 6.7 %collective-permute-start.2 = (bf16[12,128,128]{2,1,0:T(8,128)(2,1)S(1)}, bf16[12,128,128]{2,1,0:T(8,128)(2,1)S(1)}, u32[]{:S(2)}, u32[]{:S(2)}) collective-permute-start(bf16[12,128,128]{2,1,0:T(8,128)(2,1)S(1)} %get-tuple-element.18.p2), channel_id=1, source_target_pairs={{4,8},{8,4},{5,9},{9,5},{6,10},{10,6},{7,11},{11,7},{12,16},{16,12... | collective-permute-start | bytes 1179656 | tf_op jit(solution)/shard_map/ppermute | solution.py:270
  11.6 3.2 %collective-permute-start.3 = (bf16[12,128,128]{2,1,0:T(8,128)(2,1)S(1)}, bf16[12,128,128]{2,1,0:T(8,128)(2,1)S(1)}, u32[]{:S(2)}, u32[]{:S(2)}) collective-permute-start(bf16[12,128,128]{2,1,0:T(8,128)(2,1)S(1)} %get-tuple-element.19.p3), channel_id=1, source_target_pairs={{1,0},{2,1},{3,2},{4,5},{5,6},{6,7},{9,8},{10,9},{11,10},{12,13},{... | collective-permute-start | bytes 1179656 | tf_op jit(solution)/shard_map/ppermute | solution.py:270
  14.8 0.0 copy-done
  14.8 0.0 copy-done.1
  14.8 2.8 %local_slots.1 = (bf16[8,6,128,128]{3,2,1,0:T(8,128)(2,1)}, f32[6,128,128]{2,1,0:T(8,128)S(1)}) custom-call(s32[8,6]{1,0:T(8,128)S(1)} %copy-done, s32[8]{0:T(128)S(1)} %copy-done.1, bf16[8,128,128]{2,1,0:T(8,128)(2,1)S(1)} %get-tuple-element.13.diag, bf16[8,6,128,128]{3,2,1,0:T(8,128)(2,1)S(1)} %get-tuple-element.14.off, ...), custom_call_target="tpu_custom_call" | custom-call | flops 400000000 | bytes 4000000 | tf_op jit(solution)/shard_map/local_slots/pallas_call | solution.py:272
  17.7 0.0 collective-permute-done.ra
  17.7 0.0 collective-permute-done.1.rb
  17.7 1.0 %early_slots.1 = (f32[6,128,128]{2,1,0:T(8,128)S(1)}, bf16[6,2,128,128]{3,2,1,0:T(8,128)(2,1)S(1)}) custom-call(s32[8,6]{1,0:T(8,128)S(1)} %copy-done, bf16[8,6,128,128]{3,2,1,0:T(8,128)(2,1)S(1)} %get-tuple-element.14.off, f32[6,128,128]{2,1,0:T(8,128)S(1)} %get-tuple-element.21.base, bf16[12,128,128]{2,1,0:T(8,128)(2,1)S(1)} %collective-permute-done.ra, ...), custom_call_target="tpu_custom_call" | custom-call | tf_op jit(solution)/shard_map/early_slots/pallas_call | solution.py:289
  18.7 1.7 %collective-permute-done.2.ra = bf16[12,128,128]{2,1,0:T(8,128)(2,1)S(1)} collective-permute-done((bf16[12,128,128]{2,1,0:T(8,128)(2,1)S(1)}, bf16[12,128,128]{2,1,0:T(8,128)(2,1)S(1)}, u32[]{:S(2)}, u32[]{:S(2)}) %collective-permute-start.2) | collective-permute-done | bytes 393248 | tf_op jit(solution)/shard_map/ppermute | solution.py:270
  20.4 0.0 collective-permute-done.3.rb
  20.4 3.7 %second_inverses.1 = (bf16[8,128,128]{2,1,0:T(8,128)(2,1)}, bf16[8,6,128,128]{3,2,1,0:T(8,128)(2,1)}) custom-call(s32[8,6]{1,0:T(8,128)S(1)} %copy-done, s32[8]{0:T(128)S(1)} %copy-done.1, bf16[8,6,128,128]{3,2,1,0:T(8,128)(2,1)} %get-tuple-element.20.factor_in, bf16[8,6,128,128]{3,2,1,0:T(8,128)(2,1)S(1)} %get-tuple-element.14.off, ...), custom_call_target="tpu_custom_call", output_to_operand_aliasing={{1}: (2, {})} | custom-call | tf_op jit(solution)/shard_map/second_inverses/pallas_call | solution.py:298
Async XLA Ops:
  0.6 14.2 %copy-start = (s32[8,6]{1,0:T(8,128)S(1)}, s32[8,6]{1,0:T(8,128)}, u32[]{:S(2)}) copy-start(s32[8,6]{1,0:T(8,128)} %neighbors.5) | copy-start | bytes 580
  0.6 14.2 %copy-start.1 = (s32[8]{0:T(128)S(1)}, s32[8]{0:T(128)}, u32[]{:S(2)}) copy-start(s32[8]{0:T(128)} %levels.3) | copy-start | bytes 100
  3.5 14.2 %collective-permute-start = (bf16[12,128,128]{2,1,0:T(8,128)(2,1)S(1)}, bf16[12,128,128]{2,1,0:T(8,128)(2,1)S(1)}, u32[]{:S(2)}, u32[]{:S(2)}) collective-permute-start(bf16[12,128,128]{2,1,0:T(8,128)(2,1)S(1)} %get-tuple-element.16.p0), channel_id=1, source_target_pairs={{0,4},{4,0},{1,5},{5,1},{2,6},{6,2},{3,7},{7,3},{8,12},{12,8},{9,1... | collective-permute-start | bytes 1179656 | tf_op jit(solution)/shard_map/ppermute | solution.py:270
  3.6 14.0 %collective-permute-start.1 = (bf16[12,128,128]{2,1,0:T(8,128)(2,1)S(1)}, bf16[12,128,128]{2,1,0:T(8,128)(2,1)S(1)}, u32[]{:S(2)}, u32[]{:S(2)}) collective-permute-start(bf16[12,128,128]{2,1,0:T(8,128)(2,1)S(1)} %get-tuple-element.17.p1), channel_id=1, source_target_pairs={{0,1},{1,2},{2,3},{5,4},{6,5},{7,6},{8,9},{9,10},{10,11},{13,12},{... | collective-permute-start | bytes 1179656 | tf_op jit(solution)/shard_map/ppermute | solution.py:270
  4.9 15.5 %collective-permute-start.2 = (bf16[12,128,128]{2,1,0:T(8,128)(2,1)S(1)}, bf16[12,128,128]{2,1,0:T(8,128)(2,1)S(1)}, u32[]{:S(2)}, u32[]{:S(2)}) collective-permute-start(bf16[12,128,128]{2,1,0:T(8,128)(2,1)S(1)} %get-tuple-element.18.p2), channel_id=1, source_target_pairs={{4,8},{8,4},{5,9},{9,5},{6,10},{10,6},{7,11},{11,7},{12,16},{16,12... | collective-permute-start | bytes 1179656 | tf_op jit(solution)/shard_map/ppermute | solution.py:270
  11.6 8.8 %collective-permute-start.3 = (bf16[12,128,128]{2,1,0:T(8,128)(2,1)S(1)}, bf16[12,128,128]{2,1,0:T(8,128)(2,1)S(1)}, u32[]{:S(2)}, u32[]{:S(2)}) collective-permute-start(bf16[12,128,128]{2,1,0:T(8,128)(2,1)S(1)} %get-tuple-element.19.p3), channel_id=1, source_target_pairs={{1,0},{2,1},{3,2},{4,5},{5,6},{6,7},{9,8},{10,9},{11,10},{12,13},{... | collective-permute-start | bytes 1179656 | tf_op jit(solution)/shard_map/ppermute | solution.py:270

commit v3 on v2

--- a/solution.py
+++ b/solution.py
@@ -10,6 +10,8 @@
 MIRROR = (1, 0, 3, 2, 5, 4)
 VMEM_LIMIT = 40 * 1024 * 1024
 REMOTE = 4
+ROW_PAIRS = (3, 0, 3, 1, 3, 0, 3, 2)
+COL_PAIRS = ((1, 0), (2, 1), (1, 2), (2, 0), (2, 0), (1, 2), (2, 1), (1, 0))
 
 
 def dot(a, b):
@@ -72,26 +74,40 @@
     return iterates
 
 
-def slot_order():
-    row = lax.axis_index("row") % 2
-    across = 1 - row
-    return (row, 2 + row, across, 3 - row), (row, 3 - row, across, 2 + row)
+def row_colour(r):
+    return ROW_PAIRS[r % len(ROW_PAIRS)]
+
+
+def col_colour(r, c):
+    return COL_PAIRS[r % len(COL_PAIRS)][1 - c % 2]
 
 
 def transfers(rows, cols):
-    steps = [[], [], [], []]
+    steps = [[] for _ in range(REMOTE)]
     for r in range(rows):
         for c in range(cols):
             here = r * cols + c
-            up, down = (1, 3) if r % 2 == 0 else (3, 1)
+            if r + 1 < rows:
+                steps[row_colour(r)] += [(here, here + cols), (here + cols, here)]
             if c + 1 < cols:
-                steps[up].append((here, here + 1))
-            if c > 0:
-                steps[down].append((here, here - 1))
-            if r + 1 < rows:
-                pair = [(here, here + cols), (here + cols, here)]
-                steps[0 if r % 2 == 0 else 2].extend(pair)
+                steps[col_colour(r, c)] += [(here, here + 1), (here + 1, here)]
     return steps
+
+
+def slot_order():
+    period = len(ROW_PAIRS)
+    row = lax.rem(lax.axis_index("row"), period)
+    col = lax.rem(lax.axis_index("col"), 2)
+    code = jnp.int32(0)
+    for r in range(period):
+        packed = 0
+        for c in range(2):
+            colours = (row_colour(r), row_colour(r + period - 1), col_colour(r, c), col_colour(r, c + 1))
+            for slot, j in enumerate(colours):
+                packed |= slot << (8 * c + 2 * j)
+        code = jnp.where(row == r, jnp.int32(packed), code)
+    code = lax.shift_right_logical(code, 8 * col)
+    return tuple(lax.shift_right_logical(code, 2 * j) & 3 for j in range(REMOTE))
 
 
 def masked(block, named):
@@ -100,102 +116,91 @@
 
 def first_kernel(capacity, diag_hbm, off_hbm, *rest):
     payloads, (inverse, diag, off, sems) = rest[:REMOTE], rest[REMOTE:]
-    slots, _ = slot_order()
-    copy_diag = pltpu.make_async_copy(diag_hbm, diag, sems.at[0])
-    copy_off = pltpu.make_async_copy(off_hbm, off, sems.at[1])
-    copy_diag.start()
-    copy_off.start()
-    copy_diag.wait()
+    copies = [pltpu.make_async_copy(diag_hbm, diag, sems.at[0])]
+    for j, slot in enumerate(slot_order()):
+        source = off_hbm.at[pl.ds(0, capacity), slot]
+        copies.append(pltpu.make_async_copy(source, payloads[j].at[pl.ds(capacity, capacity)], sems.at[1 + j]))
+    copies.append(pltpu.make_async_copy(off_hbm, off, sems.at[1 + REMOTE]))
+    for copy in copies:
+        copy.start()
+    copies[0].wait()
     inverses = approx_inverses([diag[n].astype(jnp.float32) for n in range(capacity)], True)
-    inverses = [value.astype(jnp.bfloat16) for value in inverses]
-    copy_off.wait()
     for n in range(capacity):
-        inverse[n] = inverses[n]
-        for j in range(0, REMOTE, 2):
-            scaled = dot(inverses[n], jnp.concatenate([off[n, slots[j]], off[n, slots[j + 1]]], axis=1))
+        value = inverses[n].astype(jnp.bfloat16)
+        inverse[n] = value
+        for payload in payloads:
+            payload[n] = value
+    for copy in copies[1:]:
+        copy.wait()
+
+
+def pair_sums(blocks, inverses, uppers):
+    lowers = [dot(block, inverse).astype(jnp.bfloat16) for block, inverse in zip(blocks, inverses)]
+    return lowers, dot(jnp.concatenate(lowers, axis=1), jnp.concatenate(uppers, axis=0))
+
+
+def local_kernel(
+    capacity, rows, neighbors, levels, diag, off, inverse, factor_hbm, base, lower, scaled, sems,
+):
+    start = rows - capacity
+    slots = off.shape[1]
+    for n in range(capacity):
+        for k in range(0, slots, 2):
+            both = dot(inverse[n], jnp.concatenate([off[n, k], off[n, k + 1]], axis=1))
             for i in range(2):
-                payloads[j + i][n] = inverses[n]
-                payloads[j + i][capacity + n] = scaled[:, i * 128 : (i + 1) * 128].astype(jnp.bfloat16)
-
-
-def local_kernel(
-    capacity, rows, neighbors, levels, diag, off, inverse, p0, p1, p2, p3,
-    factor_hbm, base, lower, scaled, nothing, sems,
-):
-    payloads = (p0, p1, p2, p3)
-    slots, _ = slot_order()
-    start = rows - capacity
-    nothing[...] = jnp.zeros_like(nothing)
-
-    def each_remote(act):
-        for n in range(capacity):
-
-            @pl.when(levels[n] == 0)
-            def _():
-                for j in range(REMOTE):
-                    target = factor_hbm.at[n, slots[j]]
-
-                    @pl.when(neighbors[n, slots[j]] >= 0)
-                    def _():
-                        act(pltpu.make_async_copy(payloads[j].at[capacity + n], target, sems.at[0]))
-
-                    @pl.when(neighbors[n, slots[j]] < 0)
-                    def _():
-                        act(pltpu.make_async_copy(nothing, target, sems.at[0]))
-
-    each_remote(lambda c: c.start())
-    for n in range(capacity):
-        both = dot(inverse[n], jnp.concatenate([off[n, REMOTE], off[n, REMOTE + 1]], axis=1))
-        for i in range(2):
-            part = both[:, i * 128 : (i + 1) * 128]
-            scaled[n, i] = masked(part, neighbors[n, REMOTE + i]).astype(jnp.bfloat16)
+                part = both[:, i * 128 : (i + 1) * 128]
+                scaled[n, k + i] = masked(part, neighbors[n, k + i]).astype(jnp.bfloat16)
 
     def local_row(t, carry):
         q = start + t
-        total = diag[q].astype(jnp.float32)
+        blocks, inverses, uppers = [], [], []
         for i in range(2):
             named = neighbors[q, REMOTE + i]
-            place = jnp.clip(named % rows, 0, capacity - 1)
-            block = masked(off[q, REMOTE + i], named)
-            both = dot(block, jnp.concatenate([inverse[place], scaled[place, 1 - i]], axis=1))
-            lower[t, i] = both[:, :128].astype(jnp.bfloat16)
-            total = total - both[:, 128:]
-        base[t] = total
+            place = jnp.clip(lax.rem(named, rows), 0, capacity - 1)
+            blocks.append(masked(off[q, REMOTE + i], named))
+            inverses.append(inverse[place])
+            uppers.append(off[place, REMOTE + 1 - i])
+        lowers, total = pair_sums(blocks, inverses, uppers)
+        for i in range(2):
+            lower[t, i] = lowers[i]
+        base[t] = diag[q].astype(jnp.float32) - total
         return carry
 
     lax.fori_loop(0, capacity, local_row, 0)
 
-    def each_local(act):
+    def each(act):
         for n in range(rows):
-            target = factor_hbm.at[n, pl.ds(REMOTE, 2)]
             if n < capacity:
 
                 @pl.when(levels[n] == 0)
                 def _():
-                    act(pltpu.make_async_copy(scaled.at[n], target, sems.at[1]))
+                    act(pltpu.make_async_copy(scaled.at[n], factor_hbm.at[n], sems.at[0]))
 
             if n >= start:
 
                 @pl.when(levels[n] == 1)
                 def _():
+                    target = factor_hbm.at[n, pl.ds(REMOTE, 2)]
                     act(pltpu.make_async_copy(lower.at[n - start], target, sems.at[1]))
 
-    each_local(lambda c: c.start())
-    each_remote(lambda c: c.wait())
-    each_local(lambda c: c.wait())
+    each(lambda c: c.start())
+    each(lambda c: c.wait())
 
 
 def take(capacity, rows, t, arrived, neighbors, off, received, lower, total):
-    _, slots = slot_order()
+    slots = slot_order()
     q = rows - capacity + t
+    blocks, inverses, uppers = [], [], []
     for i, j in enumerate(arrived):
         named = neighbors[q, slots[j]]
-        place = jnp.clip(named % rows, 0, capacity - 1)
-        block = masked(off[q, slots[j]], named)
-        both = dot(block, jnp.concatenate([received[i][place], received[i][capacity + place]], axis=1))
-        lower[t, i] = both[:, :128].astype(jnp.bfloat16)
-        total = total - both[:, 128:]
-    return total
+        place = jnp.clip(lax.rem(named, rows), 0, capacity - 1)
+        blocks.append(masked(off[q, slots[j]], named))
+        inverses.append(received[i][place])
+        uppers.append(received[i][capacity + place])
+    lowers, gained = pair_sums(blocks, inverses, uppers)
+    for i in range(len(arrived)):
+        lower[t, i] = lowers[i]
+    return total - gained
 
 
 def early_kernel(capacity, rows, arrived, neighbors, off, base, ra, rb, total, lower):
@@ -208,7 +213,7 @@
     pivot, factor_hbm, lower, sems,
 ):
     del factor_in
-    _, slots = slot_order()
+    slots = slot_order()
     start = rows - capacity
 
     def each_lower(source, which, sem, act):
@@ -261,7 +266,7 @@
         ],
         in_specs=[hbm, hbm],
         out_specs=[vmem] * (REMOTE + 3),
-        scratch_shapes=[pltpu.SemaphoreType.DMA((2,))],
+        scratch_shapes=[pltpu.SemaphoreType.DMA((REMOTE + 2,))],
         compiler_params=params,
         name="first_inverses",
     )(diag_blocks, off_blocks)
@@ -272,18 +277,17 @@
     factor, base = pl.pallas_call(
         functools.partial(local_kernel, capacity, rows),
         out_shape=[factors, totals],
-        in_specs=[smem, smem] + [vmem] * (REMOTE + 3),
+        in_specs=[smem, smem] + [vmem] * 3,
         out_specs=[hbm, vmem],
         scratch_shapes=[
             pltpu.VMEM((capacity, 2, size, size), bf16),
-            pltpu.VMEM((capacity, 2, size, size), bf16),
-            pltpu.VMEM((size, size), bf16),
+            pltpu.VMEM((capacity, slots, size, size), bf16),
             pltpu.SemaphoreType.DMA((2,)),
         ],
         compiler_params=params,
         cost_estimate=pl.CostEstimate(flops=400_000_000, bytes_accessed=4_000_000, transcendentals=0),
         name="local_slots",
-    )(neighbors, levels, diag, off, inverse, *payloads)
+    )(neighbors, levels, diag, off, inverse)
 
     before, after = (0, 1), (2, 3)
     total, lower = pl.pallas_call(

time: 24.2 us -> 22.5 us (0.930)
  the two profiles are of different devices: /device:TPU:1 before, /device:TPU:17 now
where the time goes in v3:
time: 22.5 us; the launch traced here: 22.3 us
  Pallas kernels  11.1 us (49%)
  starting transfers between devices  7.02 us (31%)
  waiting for transfers between devices  3.45 us (15%)
  between operations  0.72 us (3%)
    ppermute x4, starting transfers between devices, shards(): lax.ppermute(payloads[j], ('row', 'col'), steps[j])  7.02 us
    pallas_call x1, Pallas kernels, shards(): pl.pallas_call(functools.partial(local_kernel, capacity, rows), out_shape...  3.87 us
    pallas_call x1, Pallas kernels, shards(): pl.pallas_call(functools.partial(second_kernel, capacity, rows, before, a...  3.68 us
    ppermute x4, waiting for transfers between devices, shards(): lax.ppermute(payloads[j], ('row', 'col'), steps[j])  3.45 us
    pallas_call x1, Pallas kernels, shards(): pl.pallas_call(functools.partial(first_kernel, capacity), out_shape=[payl...  2.47 us
    pallas_call x1, Pallas kernels, shards(): pl.pallas_call(functools.partial(early_kernel, capacity, rows, before), o...  1.1 us
  transfers between devices with their start and end apart: 4, of which 2 were waited for; matrix products, arithmetic and copies ran while one was open for 0% of the time, Pallas kernels for 22%

profile of v3, /device:TPU:17, one launch (start us, length us, event | category | flops | bytes accessed | tf_op | source)
XLA Modules:
  0.0 22.3 jit_solution(14446017165629474299)
XLA Ops:
  0.6 0.0 copy-start
  0.6 0.0 copy-start.1
  0.7 2.5 %first_inverses.1 = (bf16[12,128,128]{2,1,0:T(8,128)(2,1)S(1)}, bf16[12,128,128]{2,1,0:T(8,128)(2,1)S(1)}, bf16[12,128,128]{2,1,0:T(8,128)(2,1)S(1)}, bf16[12,12...) custom-call(bf16[8,128,128]{2,1,0:T(8,128)(2,1)} %diag_hbm.1, ...), custom_call_target="tpu_custom_call" | custom-call | tf_op jit(solution)/shard_map/first_inverses/pallas_call | solution.py:259
  3.1 1.8 %collective-permute-start = (bf16[12,128,128]{2,1,0:T(8,128)(2,1)S(1)}, bf16[12,128,128]{2,1,0:T(8,128)(2,1)S(1)}, u32[]{:S(2)}, u32[]{:S(2)}) collective-permute-start(bf16[12,128,128]{2,1,0:T(8,128)(2,1)S(1)} %get-tuple-element.18), channel_id=1, source_target_pairs={{0,1},{1,0},{2,3},{3,2},{4,8},{8,4},{5,9},{9,5},{6,10},{10,6},{7,1... | collective-permute-start | bytes 1179656 | tf_op jit(solution)/shard_map/ppermute | solution.py:275
  5.0 3.2 %collective-permute-start.1 = (bf16[12,128,128]{2,1,0:T(8,128)(2,1)S(1)}, bf16[12,128,128]{2,1,0:T(8,128)(2,1)S(1)}, u32[]{:S(2)}, u32[]{:S(2)}) collective-permute-start(bf16[12,128,128]{2,1,0:T(8,128)(2,1)S(1)} %get-tuple-element.19), channel_id=1, source_target_pairs={{1,2},{2,1},{4,5},{5,4},{6,7},{7,6},{9,10},{10,9},{12,16},{16,12},... | collective-permute-start | bytes 1179656 | tf_op jit(solution)/shard_map/ppermute | solution.py:275
  8.2 1.9 %collective-permute-start.2 = (bf16[12,128,128]{2,1,0:T(8,128)(2,1)S(1)}, bf16[12,128,128]{2,1,0:T(8,128)(2,1)S(1)}, u32[]{:S(2)}, u32[]{:S(2)}) collective-permute-start(bf16[12,128,128]{2,1,0:T(8,128)(2,1)S(1)} %get-tuple-element.22), channel_id=1, source_target_pairs={{5,6},{6,5},{8,9},{9,8},{10,11},{11,10},{13,14},{14,13},{17,18},{1... | collective-permute-start | bytes 1179656 | tf_op jit(solution)/shard_map/ppermute | solution.py:275
  10.1 0.1 collective-permute-start.3
  10.2 0.0 copy-done
  10.2 0.0 copy-done.1
  10.2 3.9 %local_slots.1 = (bf16[8,6,128,128]{3,2,1,0:T(8,128)(2,1)}, f32[6,128,128]{2,1,0:T(8,128)S(1)}) custom-call(s32[8,6]{1,0:T(8,128)S(1)} %copy-done, s32[8]{0:T(128)S(1)} %copy-done.1, bf16[8,128,128]{2,1,0:T(8,128)(2,1)S(1)} %get-tuple-element.13.diag, bf16[8,6,128,128]{3,2,1,0:T(8,128)(2,1)S(1)} %get-tuple-element.14.off, ...), custom_call_target="tpu_custom_call" | custom-call | flops 400000000 | bytes 4000000 | tf_op jit(solution)/shard_map/local_slots/pallas_call | solution.py:277
  14.1 0.0 collective-permute-done.ra
  14.1 1.4 %collective-permute-done.1.rb = bf16[12,128,128]{2,1,0:T(8,128)(2,1)S(1)} collective-permute-done((bf16[12,128,128]{2,1,0:T(8,128)(2,1)S(1)}, bf16[12,128,128]{2,1,0:T(8,128)(2,1)S(1)}, u32[]{:S(2)}, u32[]{:S(2)}) %collective-permute-start.1) | collective-permute-done | bytes 393248 | tf_op jit(solution)/shard_map/ppermute | solution.py:275
  15.5 1.1 %early_slots.1 = (f32[6,128,128]{2,1,0:T(8,128)S(1)}, bf16[6,2,128,128]{3,2,1,0:T(8,128)(2,1)S(1)}) custom-call(s32[8,6]{1,0:T(8,128)S(1)} %copy-done, bf16[8,6,128,128]{3,2,1,0:T(8,128)(2,1)S(1)} %get-tuple-element.14.off, f32[6,128,128]{2,1,0:T(8,128)S(1)} %get-tuple-element.17.base, bf16[12,128,128]{2,1,0:T(8,128)(2,1)S(1)} %collective-permute-done.ra, ...), custom_call_target="tpu_custom_call" | custom-call | tf_op jit(solution)/shard_map/early_slots/pallas_call | solution.py:293
  16.6 2.1 %collective-permute-done.2.ra = bf16[12,128,128]{2,1,0:T(8,128)(2,1)S(1)} collective-permute-done((bf16[12,128,128]{2,1,0:T(8,128)(2,1)S(1)}, bf16[12,128,128]{2,1,0:T(8,128)(2,1)S(1)}, u32[]{:S(2)}, u32[]{:S(2)}) %collective-permute-start.2) | collective-permute-done | bytes 393248 | tf_op jit(solution)/shard_map/ppermute | solution.py:275
  18.6 0.0 collective-permute-done.3.rb
  18.6 3.7 %second_inverses.1 = (bf16[8,128,128]{2,1,0:T(8,128)(2,1)}, bf16[8,6,128,128]{3,2,1,0:T(8,128)(2,1)}) custom-call(s32[8,6]{1,0:T(8,128)S(1)} %copy-done, s32[8]{0:T(128)S(1)} %copy-done.1, bf16[8,6,128,128]{3,2,1,0:T(8,128)(2,1)} %get-tuple-element.16.factor_in, bf16[8,6,128,128]{3,2,1,0:T(8,128)(2,1)S(1)} %get-tuple-element.14.off, ...), custom_call_target="tpu_custom_call", output_to_operand_aliasing={{1}: (2, {})} | custom-call | tf_op jit(solution)/shard_map/second_inverses/pallas_call | solution.py:302
Async XLA Ops:
  0.6 9.5 %copy-start = (s32[8,6]{1,0:T(8,128)S(1)}, s32[8,6]{1,0:T(8,128)}, u32[]{:S(2)}) copy-start(s32[8,6]{1,0:T(8,128)} %neighbors.5) | copy-start | bytes 580
  0.6 9.5 %copy-start.1 = (s32[8]{0:T(128)S(1)}, s32[8]{0:T(128)}, u32[]{:S(2)}) copy-start(s32[8]{0:T(128)} %levels.3) | copy-start | bytes 100
  3.1 10.9 %collective-permute-start = (bf16[12,128,128]{2,1,0:T(8,128)(2,1)S(1)}, bf16[12,128,128]{2,1,0:T(8,128)(2,1)S(1)}, u32[]{:S(2)}, u32[]{:S(2)}) collective-permute-start(bf16[12,128,128]{2,1,0:T(8,128)(2,1)S(1)} %get-tuple-element.18), channel_id=1, source_target_pairs={{0,1},{1,0},{2,3},{3,2},{4,8},{8,4},{5,9},{9,5},{6,10},{10,6},{7,1... | collective-permute-start | bytes 1179656 | tf_op jit(solution)/shard_map/ppermute | solution.py:275
  5.0 10.5 %collective-permute-start.1 = (bf16[12,128,128]{2,1,0:T(8,128)(2,1)S(1)}, bf16[12,128,128]{2,1,0:T(8,128)(2,1)S(1)}, u32[]{:S(2)}, u32[]{:S(2)}) collective-permute-start(bf16[12,128,128]{2,1,0:T(8,128)(2,1)S(1)} %get-tuple-element.19), channel_id=1, source_target_pairs={{1,2},{2,1},{4,5},{5,4},{6,7},{7,6},{9,10},{10,9},{12,16},{16,12},... | collective-permute-start | bytes 1179656 | tf_op jit(solution)/shard_map/ppermute | solution.py:275
  8.2 10.5 %collective-permute-start.2 = (bf16[12,128,128]{2,1,0:T(8,128)(2,1)S(1)}, bf16[12,128,128]{2,1,0:T(8,128)(2,1)S(1)}, u32[]{:S(2)}, u32[]{:S(2)}) collective-permute-start(bf16[12,128,128]{2,1,0:T(8,128)(2,1)S(1)} %get-tuple-element.22), channel_id=1, source_target_pairs={{5,6},{6,5},{8,9},{9,8},{10,11},{11,10},{13,14},{14,13},{17,18},{1... | collective-permute-start | bytes 1179656 | tf_op jit(solution)/shard_map/ppermute | solution.py:275
  10.1 8.5 %collective-permute-start.3 = (bf16[12,128,128]{2,1,0:T(8,128)(2,1)S(1)}, bf16[12,128,128]{2,1,0:T(8,128)(2,1)S(1)}, u32[]{:S(2)}, u32[]{:S(2)}) collective-permute-start(bf16[12,128,128]{2,1,0:T(8,128)(2,1)S(1)} %get-tuple-element.23), channel_id=1, source_target_pairs={{0,4},{4,0},{1,5},{5,1},{2,6},{6,2},{3,7},{7,3},{8,12},{12,8},{9,1... | collective-permute-start | bytes 1179656 | tf_op jit(solution)/shard_map/ppermute | solution.py:275

commit v4 on v3

v4 whole, which is shorter than its diff:
```python
import functools
import jax
import jax.numpy as jnp
from jax import lax
from jax.experimental import pallas as pl
from jax.experimental.pallas import tpu as pltpu
from jax.sharding import PartitionSpec as P

NS_STEPS = 4
MIRROR = (1, 0, 3, 2, 5, 4)
VMEM_LIMIT = 40 * 1024 * 1024
REMOTE = 4
ROW_PAIRS = (3, 0, 3, 1)
COL_PAIRS = ((2, 0), (1, 2), (1, 2), (2, 0))


def dot(a, b):
    return jnp.dot(a, b, preferred_element_type=jnp.float32)


def dot_t(a, b):
    return lax.dot_general(a, b, (((1,), (1,)), ((), ())), preferred_element_type=jnp.float32)


def halves(value):
    high = value.astype(jnp.bfloat16)
    low = (value - high.astype(jnp.float32)).astype(jnp.bfloat16)
    return high, low


def approx_inverses(matrices, exact):
    size = matrices[0].shape[0]
    eye = (
        lax.broadcasted_iota(jnp.int32, (size, size), 0)
        == lax.broadcasted_iota(jnp.int32, (size, size), 1)
    ).astype(jnp.float32)
    iterates, residuals = [], []
    for matrix in matrices:
        turned = matrix.T
        column = jnp.max(jnp.sum(jnp.abs(matrix), axis=0, keepdims=True), axis=1, keepdims=True)
        row = jnp.max(jnp.sum(jnp.abs(turned), axis=0, keepdims=True), axis=1, keepdims=True)
        scale = 1.0 / (column * row)
        if exact:
            square = dot_t(matrix.astype(jnp.bfloat16), matrix.astype(jnp.bfloat16))
        else:
            high, low = halves(matrix)
            left = jnp.concatenate([high, low], axis=1)
            right = jnp.concatenate(
                [
                    jnp.concatenate([high, high], axis=1),
                    jnp.concatenate([low, low], axis=1),
                ],
                axis=0,
            )
            both = dot_t(left, right)
            square = both[:, :size] + both[:, size:]
        iterates.append(turned * scale)
        residuals.append(eye - square * scale)
    for step in range(NS_STEPS):
        last = step == NS_STEPS - 1
        for n in range(len(matrices)):
            r_high, r_low = halves(residuals[n])
            x_high, x_low = halves(iterates[n])
            row = jnp.concatenate([r_high, r_low], axis=1)
            right = jnp.concatenate([row, row], axis=0)
            left = jnp.concatenate([x_high, x_low], axis=1)
            if not last:
                left = jnp.concatenate([row, left], axis=0)
            both = dot(left, right)
            both = both[:, :size] + both[:, size:]
            iterates[n] = iterates[n] + both[-size:]
            if not last:
                residuals[n] = both[:size]
    return iterates


def row_colour(r):
    return ROW_PAIRS[r % len(ROW_PAIRS)]


def col_colour(r, c):
    return COL_PAIRS[r % len(COL_PAIRS)][1 - c % 2]


def transfers(rows, cols):
    steps = [[] for _ in range(REMOTE)]
    for r in range(rows):
        for c in range(cols):
            here = r * cols + c
            if r + 1 < rows:
                steps[row_colour(r)] += [(here, here + cols), (here + cols, here)]
            if c + 1 < cols:
                steps[col_colour(r, c)] += [(here, here + 1), (here + 1, here)]
    return steps


def slot_order():
    period = len(ROW_PAIRS)
    row = lax.rem(lax.axis_index("row"), period)
    col = lax.rem(lax.axis_index("col"), 2)
    code = jnp.int32(0)
    for r in range(period):
        packed = 0
        for c in range(2):
            colours = (row_colour(r), row_colour(r + period - 1), col_colour(r, c), col_colour(r, c + 1))
            for slot, j in enumerate(colours):
                packed |= slot << (8 * c + 2 * j)
        code = jnp.where(row == r, jnp.int32(packed), code)
    code = lax.shift_right_logical(code, 8 * col)
    return tuple(lax.shift_right_logical(code, 2 * j) & 3 for j in range(REMOTE))


def masked(block, named):
    return jnp.where(named >= 0, block, jnp.zeros_like(block))


def first_kernel(
    capacity, rows, neighbors_hbm, levels_hbm, diag_hbm, off_hbm, p0, p1, p2, p3, inverse, diag, off,
    neighbors, levels, places, sems,
):
    payloads = (p0, p1, p2, p3)
    slots = slot_order()
    start = rows - capacity
    copies = [
        pltpu.make_async_copy(neighbors_hbm, neighbors, sems.at[0]),
        pltpu.make_async_copy(levels_hbm, levels, sems.at[1]),
        pltpu.make_async_copy(diag_hbm, diag, sems.at[2]),
        pltpu.make_async_copy(off_hbm, off, sems.at[3]),
    ]
    for copy in copies:
        copy.start()
    copies[0].wait()
    copies[1].wait()
    for j in range(REMOTE):
        for t in range(capacity):
            places[j * rows + t] = 0
        for n in range(capacity):
            named = neighbors[n, slots[j]]
            live = jnp.logical_and(named >= 0, levels[n] == 0)
            places[j * rows + jnp.where(live, lax.rem(named, rows) - start, capacity)] = n
    for j in range(REMOTE):
        for t in range(capacity):
            pltpu.make_async_copy(
                off_hbm.at[places[j * rows + t], slots[j]], payloads[j].at[capacity + t], sems.at[4 + j]
            ).start()
    copies[2].wait()
    inverses = approx_inverses([diag[n].astype(jnp.float32) for n in range(capacity)], True)
    for n in range(capacity):
        inverse[n] = inverses[n].astype(jnp.bfloat16)

    def pack(t, carry):
        for j in range(REMOTE):
            payloads[j][t] = inverse[places[j * rows + t]]
        return carry

    lax.fori_loop(0, capacity, pack, 0)
    copies[3].wait()
    for j in range(REMOTE):
        whole = payloads[j].at[pl.ds(capacity, capacity)]
        pltpu.make_async_copy(off_hbm.at[pl.ds(0, capacity), 0], whole, sems.at[4 + j]).wait()


def pair_sums(blocks, inverses, uppers):
    lowers = [dot(block, inverse).astype(jnp.bfloat16) for block, inverse in zip(blocks, inverses)]
    return lowers, dot(jnp.concatenate(lowers, axis=1), jnp.concatenate(uppers, axis=0))


def local_kernel(
    capacity, rows, neighbors, levels, diag, off, inverse, factor_hbm, base, remote, kept, late, lower, scaled, sems,
):
    start = rows - capacity
    slots = off.shape[1]
    order = slot_order()
    for n in range(capacity):
        for k in range(0, slots, 2):
            both = dot(inverse[n], jnp.concatenate([off[n, k], off[n, k + 1]], axis=1))
            for i in range(2):
                part = masked(both[:, i * 128 : (i + 1) * 128], neighbors[n, k + i]).astype(jnp.bfloat16)
                scaled[n, k + i] = part
                if n >= start and k < REMOTE:
                    kept[n - start, k + i] = part

    def local_row(t, carry):
        q = start + t
        blocks, inverses, uppers = [], [], []
        for i in range(2):
            named = neighbors[q, REMOTE + i]
            place = jnp.clip(lax.rem(named, rows), 0, capacity - 1)
            blocks.append(masked(off[q, REMOTE + i], named))
            inverses.append(inverse[place])
            uppers.append(off[place, REMOTE + 1 - i])
        lowers, total = pair_sums(blocks, inverses, uppers)
        for i in range(2):
            lower[t, i] = lowers[i]
        base[t] = diag[q].astype(jnp.float32) - total
        for j in range(REMOTE):
            live = jnp.where(levels[q] == 1, neighbors[q, order[j]], -1)
            remote[j, t] = masked(off[q, order[j]], live)
        late[t] = jnp.full(late.shape[1:], levels[q].astype(jnp.float32))
        return carry

    lax.fori_loop(0, capacity, local_row, 0)

    def each(act):
        for n in range(rows):
            if n < start:
                act(pltpu.make_async_copy(scaled.at[n], factor_hbm.at[n], sems.at[0]))
                continue
            target = factor_hbm.at[n, pl.ds(REMOTE, 2)]

            @pl.when(levels[n] == 1)
            def _():
                act(pltpu.make_async_copy(lower.at[n - start], target, sems.at[1]))

            if n < capacity:

                @pl.when(levels[n] == 0)
                def _():
                    act(pltpu.make_async_copy(scaled.at[n, pl.ds(REMOTE, 2)], target, sems.at[1]))

    each(lambda c: c.start())
    each(lambda c: c.wait())


def take(capacity, t, arrived, remote, received, late, kept, total):
    order = slot_order()
    lowers, gained = pair_sums(
        [remote[j, t] for j in arrived],
        [blocks[t] for blocks in received],
        [blocks[capacity + t] for blocks in received],
    )
    is_late = late[t][:1] > 0.5
    for j, lower in zip(arrived, lowers):
        kept[t, order[j]] = jnp.where(is_late, lower, kept[t, order[j]])
    return total - gained


def early_kernel(capacity, arrived, remote, base, late, kept_in, ra, rb, total, kept):
    del kept_in
    for t in range(capacity):
        total[t] = take(capacity, t, arrived, remote, (ra, rb), late, kept, base[t])


def second_kernel(
    capacity, rows, arrived, factor_in, kept_in, inverse, total, remote, late, ra, rb, pivot, factor_hbm, kept, sem,
):
    del factor_in, kept_in
    start = rows - capacity
    pivots = [take(capacity, t, arrived, remote, (ra, rb), late, kept, total[t]) for t in range(capacity)]
    copy = pltpu.make_async_copy(kept, factor_hbm.at[pl.ds(start, capacity), pl.ds(0, REMOTE)], sem)
    copy.start()
    inverses = approx_inverses(pivots, False)
    for n in range(rows):
        if n < start:
            pivot[n] = inverse[n]
            continue
        value = inverses[n - start].astype(jnp.bfloat16)
        if n < capacity:
            value = jnp.where(late[n - start][:1] > 0.5, value, inverse[n])
        pivot[n] = value
    copy.wait()


def shards(diag_blocks, off_blocks, neighbors, levels):
    rows, slots = off_blocks.shape[:2]
    size = diag_blocks.shape[1]
    capacity = 3 * rows // 4
    smem = pl.BlockSpec(memory_space=pltpu.SMEM)
    vmem = pl.BlockSpec(memory_space=pltpu.VMEM)
    hbm = pl.BlockSpec(memory_space=pltpu.HBM)
    params = pltpu.CompilerParams(vmem_limit_bytes=VMEM_LIMIT)
    bf16 = jnp.bfloat16
    payload = jax.ShapeDtypeStruct((2 * capacity, size, size), bf16)
    totals = jax.ShapeDtypeStruct((capacity, size, size), jnp.float32)
    factors = jax.ShapeDtypeStruct(off_blocks.shape, bf16)
    pivots = jax.ShapeDtypeStruct((rows, size, size), bf16)
    kepts = jax.ShapeDtypeStruct((capacity, REMOTE, size, size), bf16)

    diag_blocks, off_blocks, neighbors, levels = (
        pltpu.with_memory_space_constraint(value, pltpu.HBM)
        for value in (diag_blocks, off_blocks, neighbors, levels)
    )
    *payloads, inverse, diag, off = pl.pallas_call(
        functools.partial(first_kernel, capacity, rows),
        out_shape=[payload] * REMOTE + [jax.ShapeDtypeStruct((capacity, size, size), bf16), pivots, factors],
        in_specs=[hbm] * 4,
        out_specs=[vmem] * (REMOTE + 3),
        scratch_shapes=[
            pltpu.SMEM(neighbors.shape, jnp.int32),
            pltpu.SMEM(levels.shape, jnp.int32),
            pltpu.SMEM((REMOTE * rows,), jnp.int32),
            pltpu.SemaphoreType.DMA((4 + REMOTE,)),
        ],
        compiler_params=params,
        name="first_inverses",
    )(neighbors, levels, diag_blocks, off_blocks)

    steps = transfers(lax.axis_size("row"), lax.axis_size("col"))
    received = [lax.ppermute(payloads[j], ("row", "col"), steps[j]) for j in range(REMOTE)]

    factor, base, remote, kept, late = pl.pallas_call(
        functools.partial(local_kernel, capacity, rows),
        out_shape=[
            factors,
            totals,
            jax.ShapeDtypeStruct((REMOTE, capacity, size, size), bf16),
            kepts,
            jax.ShapeDtypeStruct((capacity, 8, size), jnp.float32),
        ],
        in_specs=[smem, smem] + [vmem] * 3,
        out_specs=[hbm] + [vmem] * 4,
        scratch_shapes=[
            pltpu.VMEM((capacity, 2, size, size), bf16),
            pltpu.VMEM((capacity, slots, size, size), bf16),
            pltpu.SemaphoreType.DMA((2,)),
        ],
        compiler_params=params,
        cost_estimate=pl.CostEstimate(flops=400_000_000, bytes_accessed=4_000_000, transcendentals=0),
        name="local_slots",
    )(neighbors, levels, diag, off, inverse)

    before, after = (0, 1), (2, 3)
    total, kept = pl.pallas_call(
        functools.partial(early_kernel, capacity, before),
        out_shape=[totals, kepts],
        in_specs=[vmem] * 6,
        out_specs=[vmem, vmem],
        input_output_aliases={3: 1},
        compiler_params=params,
        name="early_slots",
    )(remote, base, late, kept, *(received[j] for j in before))

    pivot, factor, _ = pl.pallas_call(
        functools.partial(second_kernel, capacity, rows, after),
        out_shape=[pivots, factors, kepts],
        in_specs=[hbm] + [vmem] * 7,
        out_specs=[vmem, hbm, vmem],
        scratch_shapes=[pltpu.SemaphoreType.DMA],
        input_output_aliases={0: 1, 1: 2},
        compiler_params=params,
        name="second_inverses",
    )(factor, kept, inverse, total, remote, late, *(received[j] for j in after))
    return (pivot, factor)


def solution(mesh):
    in_specs = (
        P(("row", "col"), None, None),
        P(("row", "col"), None, None, None),
        P(("row", "col"), None),
        P(("row", "col")),
    )
    out_specs = (P(("row", "col"), None, None), P(("row", "col"), None, None, None))
    return jax.shard_map(shards, mesh=mesh, in_specs=in_specs, out_specs=out_specs, check_vma=False)
```

time: 22.5 us -> 20.2 us (0.90)
  the two profiles are of different devices: /device:TPU:17 before, /device:TPU:12 now
where the time goes in v4:
time: 20.2 us; the launch traced here: 20 us
  Pallas kernels  9.07 us (45%)
  starting transfers between devices  7.7 us (38%)
  waiting for transfers between devices  2.55 us (13%)
  between operations  0.69 us (3%)
    ppermute x4, starting transfers between devices, shards(): lax.ppermute(payloads[j], ('row', 'col'), steps[j])  7.7 us
    pallas_call x1, Pallas kernels, shards(): pl.pallas_call(functools.partial(local_kernel, capacity, rows), out_shape...  3.81 us
    ppermute x4, waiting for transfers between devices, shards(): lax.ppermute(payloads[j], ('row', 'col'), steps[j])  2.55 us
    pallas_call x1, Pallas kernels, shards(): pl.pallas_call(functools.partial(first_kernel, capacity, rows), out_shape...  2.49 us
    pallas_call x1, Pallas kernels, shards(): pl.pallas_call(functools.partial(second_kernel, capacity, rows, after), o...  2.3 us
    pallas_call x1, Pallas kernels, shards(): pl.pallas_call(functools.partial(early_kernel, capacity, before), out_sha...  0.47 us
  transfers between devices with their start and end apart: 4, of which 1 were waited for; matrix products, arithmetic and copies ran while one was open for 0% of the time, Pallas kernels for 21%

profile of v4, /device:TPU:12, one launch (start us, length us, event | category | flops | bytes accessed | tf_op | source)
XLA Modules:
  0.0 20.0 jit_solution(9265877410546658125)
XLA Ops:
  0.6 2.5 %first_inverses.1 = (bf16[12,128,128]{2,1,0:T(8,128)(2,1)S(1)}, bf16[12,128,128]{2,1,0:T(8,128)(2,1)S(1)}, bf16[12,128,128]{2,1,0:T(8,128)(2,1)S(1)}, bf16[12,12...) custom-call(s32[8,6]{1,0:T(8,128)} %neighbors.1, ...), custom_call_target="tpu_custom_call" | custom-call | tf_op jit(solution)/shard_map/first_inverses/pallas_call | solution.py:283
  3.1 0.5 %collective-permute-start = (bf16[12,128,128]{2,1,0:T(8,128)(2,1)S(1)}, bf16[12,128,128]{2,1,0:T(8,128)(2,1)S(1)}, u32[]{:S(2)}, u32[]{:S(2)}) collective-permute-start(bf16[12,128,128]{2,1,0:T(8,128)(2,1)S(1)} %get-tuple-element.26), channel_id=1, source_target_pairs={{0,1},{1,0},{2,3},{3,2},{4,8},{8,4},{5,9},{9,5},{6,10},{10,6},{7,1... | collective-permute-start | bytes 1179656 | tf_op jit(solution)/shard_map/ppermute | solution.py:299
  3.7 2.5 %collective-permute-start.1 = (bf16[12,128,128]{2,1,0:T(8,128)(2,1)S(1)}, bf16[12,128,128]{2,1,0:T(8,128)(2,1)S(1)}, u32[]{:S(2)}, u32[]{:S(2)}) collective-permute-start(bf16[12,128,128]{2,1,0:T(8,128)(2,1)S(1)} %get-tuple-element.27), channel_id=1, source_target_pairs={{5,6},{6,5},{9,10},{10,9},{12,16},{16,12},{13,17},{17,13},{14,18},... | collective-permute-start | bytes 1179656 | tf_op jit(solution)/shard_map/ppermute | solution.py:299
  6.1 4.6 %collective-permute-start.2 = (bf16[12,128,128]{2,1,0:T(8,128)(2,1)S(1)}, bf16[12,128,128]{2,1,0:T(8,128)(2,1)S(1)}, u32[]{:S(2)}, u32[]{:S(2)}) collective-permute-start(bf16[12,128,128]{2,1,0:T(8,128)(2,1)S(1)} %get-tuple-element.30), channel_id=1, source_target_pairs={{1,2},{2,1},{4,5},{5,4},{6,7},{7,6},{8,9},{9,8},{10,11},{11,10},{1... | collective-permute-start | bytes 1179656 | tf_op jit(solution)/shard_map/ppermute | solution.py:299
  10.8 0.1 collective-permute-start.3
  10.9 3.8 %local_slots.1 = (bf16[8,6,128,128]{3,2,1,0:T(8,128)(2,1)}, f32[6,128,128]{2,1,0:T(8,128)S(1)}, bf16[4,6,128,128]{3,2,1,0:T(8,128)(2,1)S(1)}, bf16[6,4,128,128]{3,2,1,0:T(8,128)(2,1)S(1)}, f32[6,8,128]{2,1,0:T(8,128)S(1)}) custom-call(s32[8,6]{1,0:T(8,128)} %neighbors.1, s32[8]{0:T(128)} %levels.1, bf16[8,128,128]{2,1,0:T(8,128)(2,1)S(1)} %get-tuple-element.18.diag, ...), custom_call_target="tpu_custom_call" | custom-call | flops 400000000 | bytes 4000000 | tf_op jit(solution)/shard_map/local_slots/pallas_call | solution.py:301
  14.7 0.0 collective-permute-done.ra
  14.7 0.0 collective-permute-done.1.rb
  14.7 0.5 %early_slots.1 = (f32[6,128,128]{2,1,0:T(8,128)S(1)}, bf16[6,4,128,128]{3,2,1,0:T(8,128)(2,1)S(1)}) custom-call(bf16[4,6,128,128]{3,2,1,0:T(8,128)(2,1)S(1)} %get-tuple-element.22.remote, f32[6,128,128]{2,1,0:T(8,128)S(1)} %get-tuple-element.23.base, f32[6,8,128]{2,1,0:T(8,128)S(1)} %get-tuple-element.24.late, ...), custom_call_target="tpu_custom_call", output_to_operand_aliasing={{1}: (3, {})} | custom-call | tf_op jit(solution)/shard_map/early_slots/pallas_call | solution.py:323
  15.2 2.5 %collective-permute-done.2.ra = bf16[12,128,128]{2,1,0:T(8,128)(2,1)S(1)} collective-permute-done((bf16[12,128,128]{2,1,0:T(8,128)(2,1)S(1)}, bf16[12,128,128]{2,1,0:T(8,128)(2,1)S(1)}, u32[]{:S(2)}, u32[]{:S(2)}) %collective-permute-start.2) | collective-permute-done | bytes 393248 | tf_op jit(solution)/shard_map/ppermute | solution.py:299
  17.7 0.0 collective-permute-done.3.rb
  17.7 2.3 %second_inverses.1 = (bf16[8,128,128]{2,1,0:T(8,128)(2,1)}, bf16[8,6,128,128]{3,2,1,0:T(8,128)(2,1)}, bf16[6,4,128,128]{3,2,1,0:T(8,128)(2,1)S(1)}) custom-call(bf16[8,6,128,128]{3,2,1,0:T(8,128)(2,1)} %get-tuple-element.21.factor_in, bf16[6,4,128,128]{3,2,1,0:T(8,128)(2,1)S(1)} %get-tuple-element.28.kept_in, ...), custom_call_target="tpu_custom_call", output_to_operand_aliasing={{1}: (0, {}), {2}: (1, {})} | custom-call | tf_op jit(solution)/shard_map/second_inverses/pallas_call | solution.py:333
Async XLA Ops:
  3.1 11.5 %collective-permute-start = (bf16[12,128,128]{2,1,0:T(8,128)(2,1)S(1)}, bf16[12,128,128]{2,1,0:T(8,128)(2,1)S(1)}, u32[]{:S(2)}, u32[]{:S(2)}) collective-permute-start(bf16[12,128,128]{2,1,0:T(8,128)(2,1)S(1)} %get-tuple-element.26), channel_id=1, source_target_pairs={{0,1},{1,0},{2,3},{3,2},{4,8},{8,4},{5,9},{9,5},{6,10},{10,6},{7,1... | collective-permute-start | bytes 1179656 | tf_op jit(solution)/shard_map/ppermute | solution.py:299
  3.7 11.0 %collective-permute-start.1 = (bf16[12,128,128]{2,1,0:T(8,128)(2,1)S(1)}, bf16[12,128,128]{2,1,0:T(8,128)(2,1)S(1)}, u32[]{:S(2)}, u32[]{:S(2)}) collective-permute-start(bf16[12,128,128]{2,1,0:T(8,128)(2,1)S(1)} %get-tuple-element.27), channel_id=1, source_target_pairs={{5,6},{6,5},{9,10},{10,9},{12,16},{16,12},{13,17},{17,13},{14,18},... | collective-permute-start | bytes 1179656 | tf_op jit(solution)/shard_map/ppermute | solution.py:299
  6.1 11.6 %collective-permute-start.2 = (bf16[12,128,128]{2,1,0:T(8,128)(2,1)S(1)}, bf16[12,128,128]{2,1,0:T(8,128)(2,1)S(1)}, u32[]{:S(2)}, u32[]{:S(2)}) collective-permute-start(bf16[12,128,128]{2,1,0:T(8,128)(2,1)S(1)} %get-tuple-element.30), channel_id=1, source_target_pairs={{1,2},{2,1},{4,5},{5,4},{6,7},{7,6},{8,9},{9,8},{10,11},{11,10},{1... | collective-permute-start | bytes 1179656 | tf_op jit(solution)/shard_map/ppermute | solution.py:299
  10.8 6.9 %collective-permute-start.3 = (bf16[12,128,128]{2,1,0:T(8,128)(2,1)S(1)}, bf16[12,128,128]{2,1,0:T(8,128)(2,1)S(1)}, u32[]{:S(2)}, u32[]{:S(2)}) collective-permute-start(bf16[12,128,128]{2,1,0:T(8,128)(2,1)S(1)} %get-tuple-element.31), channel_id=1, source_target_pairs={{0,4},{4,0},{1,5},{5,1},{2,6},{6,2},{3,7},{7,3},{8,12},{12,8},{9,1... | collective-permute-start | bytes 1179656 | tf_op jit(solution)/shard_map/ppermute | solution.py:299

commit v5 on v4

--- a/solution.py
+++ b/solution.py
@@ -10,8 +10,22 @@
 MIRROR = (1, 0, 3, 2, 5, 4)
 VMEM_LIMIT = 40 * 1024 * 1024
 REMOTE = 4
-ROW_PAIRS = (3, 0, 3, 1)
-COL_PAIRS = ((2, 0), (1, 2), (1, 2), (2, 0))
+EVERY_DEVICE = (
+    ((6, 0, 2, 4), (6, 2, 3, 0), (6, 3, 2, 0), (0, 6, 3, 4)),
+    ((2, 1, 0, 5), (3, 2, 0, 1), (0, 3, 2, 1), (1, 0, 3, 5)),
+    ((2, 0, 1, 4), (3, 2, 1, 0), (1, 3, 0, 2), (0, 1, 4, 3)),
+    ((0, 1, 2, 5), (0, 2, 3, 1), (0, 3, 1, 2), (1, 0, 5, 3)),
+    ((1, 2, 4, 0), (1, 3, 2, 0), (1, 0, 3, 2), (0, 1, 4, 3)),
+    ((0, 2, 5, 1), (0, 3, 2, 1), (0, 1, 3, 2), (1, 0, 5, 3)),
+    ((1, 0, 2, 4), (1, 2, 3, 0), (1, 3, 2, 0), (4, 1, 3, 0)),
+    ((6, 1, 2, 5), (6, 2, 3, 1), (6, 3, 2, 1), (5, 6, 3, 1)),
+)
+ANY_MESH = (
+    ((2, 1, 3, 0), (3, 1, 2, 0)),
+    ((0, 3, 2, 1), (0, 2, 3, 1)),
+    ((1, 3, 2, 0), (1, 2, 3, 0)),
+    ((2, 0, 3, 1), (3, 0, 2, 1)),
+)
 
 
 def dot(a, b):
@@ -74,40 +88,34 @@
     return iterates
 
 
-def row_colour(r):
-    return ROW_PAIRS[r % len(ROW_PAIRS)]
-
-
-def col_colour(r, c):
-    return COL_PAIRS[r % len(COL_PAIRS)][1 - c % 2]
+def meetings(rows, cols):
+    return EVERY_DEVICE if (rows, cols) == (8, 4) else ANY_MESH
 
 
 def transfers(rows, cols):
+    plan = meetings(rows, cols)
     steps = [[] for _ in range(REMOTE)]
     for r in range(rows):
         for c in range(cols):
-            here = r * cols + c
-            if r + 1 < rows:
-                steps[row_colour(r)] += [(here, here + cols), (here + cols, here)]
-            if c + 1 < cols:
-                steps[col_colour(r, c)] += [(here, here + 1), (here + 1, here)]
+            around = ((r + 1, c), (r - 1, c), (r, c + 1), (r, c - 1), (r + 1, c), (r - 1, c), (rows - 1 - r, c))
+            entry = plan[r % len(plan)][c % len(plan[0])]
+            for j in range(REMOTE):
+                to_row, to_col = around[entry[j]]
+                if 0 <= to_row < rows and 0 <= to_col < cols:
+                    steps[j].append((r * cols + c, to_row * cols + to_col))
     return steps
 
 
 def slot_order():
-    period = len(ROW_PAIRS)
-    row = lax.rem(lax.axis_index("row"), period)
-    col = lax.rem(lax.axis_index("col"), 2)
+    plan = meetings(lax.axis_size("row"), lax.axis_size("col"))
+    row = lax.rem(lax.axis_index("row"), len(plan))
+    col = lax.rem(lax.axis_index("col"), len(plan[0]))
     code = jnp.int32(0)
-    for r in range(period):
-        packed = 0
-        for c in range(2):
-            colours = (row_colour(r), row_colour(r + period - 1), col_colour(r, c), col_colour(r, c + 1))
-            for slot, j in enumerate(colours):
-                packed |= slot << (8 * c + 2 * j)
-        code = jnp.where(row == r, jnp.int32(packed), code)
-    code = lax.shift_right_logical(code, 8 * col)
-    return tuple(lax.shift_right_logical(code, 2 * j) & 3 for j in range(REMOTE))
+    for r, line in enumerate(plan):
+        for c, entry in enumerate(line):
+            packed = sum(min(entry[j], REMOTE) << (3 * j) for j in range(REMOTE))
+            code = jnp.where(row * len(line) + col == r * len(line) + c, jnp.int32(packed), code)
+    return tuple(lax.shift_right_logical(code, 3 * j) & 7 for j in range(REMOTE))
 
 
 def masked(block, named):
@@ -194,7 +202,7 @@
             lower[t, i] = lowers[i]
         base[t] = diag[q].astype(jnp.float32) - total
         for j in range(REMOTE):
-            live = jnp.where(levels[q] == 1, neighbors[q, order[j]], -1)
+            live = jnp.where(jnp.logical_and(levels[q] == 1, order[j] < REMOTE), neighbors[q, order[j]], -1)
             remote[j, t] = masked(off[q, order[j]], live)
         late[t] = jnp.full(late.shape[1:], levels[q].astype(jnp.float32))
         return carry
@@ -247,7 +255,8 @@
     del factor_in, kept_in
     start = rows - capacity
     pivots = [take(capacity, t, arrived, remote, (ra, rb), late, kept, total[t]) for t in range(capacity)]
-    copy = pltpu.make_async_copy(kept, factor_hbm.at[pl.ds(start, capacity), pl.ds(0, REMOTE)], sem)
+    finished = kept.at[:, pl.ds(0, REMOTE)]
+    copy = pltpu.make_async_copy(finished, factor_hbm.at[pl.ds(start, capacity), pl.ds(0, REMOTE)], sem)
     copy.start()
     inverses = approx_inverses(pivots, False)
     for n in range(rows):
@@ -274,7 +283,7 @@
     totals = jax.ShapeDtypeStruct((capacity, size, size), jnp.float32)
     factors = jax.ShapeDtypeStruct(off_blocks.shape, bf16)
     pivots = jax.ShapeDtypeStruct((rows, size, size), bf16)
-    kepts = jax.ShapeDtypeStruct((capacity, REMOTE, size, size), bf16)
+    kepts = jax.ShapeDtypeStruct((capacity, REMOTE + 1, size, size), bf16)
 
     diag_blocks, off_blocks, neighbors, levels = (
         pltpu.with_memory_space_constraint(value, pltpu.HBM)

time: 20.2 us -> 18.9 us (0.936)
  the two profiles are of different devices: /device:TPU:12 before, /device:TPU:1 now
where the time goes in v5:
time: 18.9 us; the launch traced here: 18.7 us
  Pallas kernels  9.09 us (48%)
  starting transfers between devices  6.61 us (35%)
  waiting for transfers between devices  2.33 us (12%)
  between operations  0.67 us (4%)
    ppermute x4, starting transfers between devices, shards(): lax.ppermute(payloads[j], ('row', 'col'), steps[j])  6.61 us
    pallas_call x1, Pallas kernels, shards(): pl.pallas_call(functools.partial(local_kernel, capacity, rows), out_shape...  3.82 us
    pallas_call x1, Pallas kernels, shards(): pl.pallas_call(functools.partial(first_kernel, capacity, rows), out_shape...  2.5 us
    ppermute x4, waiting for transfers between devices, shards(): lax.ppermute(payloads[j], ('row', 'col'), steps[j])  2.33 us
    pallas_call x1, Pallas kernels, shards(): pl.pallas_call(functools.partial(second_kernel, capacity, rows, after), o...  2.3 us
    pallas_call x1, Pallas kernels, shards(): pl.pallas_call(functools.partial(early_kernel, capacity, before), out_sha...  0.47 us
  transfers between devices with their start and end apart: 4, of which 1 were waited for; matrix products, arithmetic and copies ran while one was open for 0% of the time, Pallas kernels for 23%

profile of v5, /device:TPU:1, one launch (start us, length us, event | category | flops | bytes accessed | tf_op | source)
XLA Modules:
  0.0 18.7 jit_solution(10956375937615462912)
XLA Ops:
  0.6 2.5 %first_inverses.1 = (bf16[12,128,128]{2,1,0:T(8,128)(2,1)S(1)}, bf16[12,128,128]{2,1,0:T(8,128)(2,1)S(1)}, bf16[12,128,128]{2,1,0:T(8,128)(2,1)S(1)}, bf16[12,12...) custom-call(s32[8,6]{1,0:T(8,128)} %neighbors.1, ...), custom_call_target="tpu_custom_call" | custom-call | tf_op jit(solution)/shard_map/first_inverses/pallas_call | solution.py:292
  3.1 2.2 %collective-permute-start = (bf16[12,128,128]{2,1,0:T(8,128)(2,1)S(1)}, bf16[12,128,128]{2,1,0:T(8,128)(2,1)S(1)}, u32[]{:S(2)}, u32[]{:S(2)}) collective-permute-start(bf16[12,128,128]{2,1,0:T(8,128)(2,1)S(1)} %get-tuple-element.26), channel_id=1, source_target_pairs={{0,28},{1,29},{2,30},{3,7},{4,5},{5,4},{6,10},{7,3},{8,9},{9,8},{1... | collective-permute-start | bytes 1179656 | tf_op jit(solution)/shard_map/ppermute | solution.py:308
  5.3 1.3 %collective-permute-start.1 = (bf16[12,128,128]{2,1,0:T(8,128)(2,1)S(1)}, bf16[12,128,128]{2,1,0:T(8,128)(2,1)S(1)}, u32[]{:S(2)}, u32[]{:S(2)}) collective-permute-start(bf16[12,128,128]{2,1,0:T(8,128)(2,1)S(1)} %get-tuple-element.27), channel_id=1, source_target_pairs={{0,4},{1,2},{2,1},{3,31},{4,0},{5,6},{6,5},{7,11},{8,12},{9,10},{1... | collective-permute-start | bytes 1179656 | tf_op jit(solution)/shard_map/ppermute | solution.py:308
  6.6 0.8 %collective-permute-start.2 = (bf16[12,128,128]{2,1,0:T(8,128)(2,1)S(1)}, bf16[12,128,128]{2,1,0:T(8,128)(2,1)S(1)}, u32[]{:S(2)}, u32[]{:S(2)}) collective-permute-start(bf16[12,128,128]{2,1,0:T(8,128)(2,1)S(1)} %get-tuple-element.30), channel_id=1, source_target_pairs={{0,1},{1,0},{2,3},{3,2},{4,8},{5,9},{6,7},{7,6},{8,4},{9,5},{10,14... | collective-permute-start | bytes 1179656 | tf_op jit(solution)/shard_map/ppermute | solution.py:308
  7.4 2.3 %collective-permute-start.3 = (bf16[12,128,128]{2,1,0:T(8,128)(2,1)S(1)}, bf16[12,128,128]{2,1,0:T(8,128)(2,1)S(1)}, u32[]{:S(2)}, u32[]{:S(2)}) collective-permute-start(bf16[12,128,128]{2,1,0:T(8,128)(2,1)S(1)} %get-tuple-element.31), channel_id=1, source_target_pairs={{0,4},{1,5},{2,6},{3,7},{4,0},{5,1},{6,2},{7,3},{8,12},{9,13},{10,... | collective-permute-start | bytes 1179656 | tf_op jit(solution)/shard_map/ppermute | solution.py:308
  9.7 3.8 %local_slots.1 = (bf16[8,6,128,128]{3,2,1,0:T(8,128)(2,1)}, f32[6,128,128]{2,1,0:T(8,128)S(1)}, bf16[4,6,128,128]{3,2,1,0:T(8,128)(2,1)S(1)}, bf16[6,5,128,128]{3,2,1,0:T(8,128)(2,1)S(1)}, f32[6,8,128]{2,1,0:T(8,128)S(1)}) custom-call(s32[8,6]{1,0:T(8,128)} %neighbors.1, s32[8]{0:T(128)} %levels.1, bf16[8,128,128]{2,1,0:T(8,128)(2,1)S(1)} %get-tuple-element.18.diag, ...), custom_call_target="tpu_custom_call" | custom-call | flops 400000000 | bytes 4000000 | tf_op jit(solution)/shard_map/local_slots/pallas_call | solution.py:310
  13.6 0.0 collective-permute-done.ra
  13.6 0.0 collective-permute-done.1.rb
  13.6 0.5 %early_slots.1 = (f32[6,128,128]{2,1,0:T(8,128)S(1)}, bf16[6,5,128,128]{3,2,1,0:T(8,128)(2,1)S(1)}) custom-call(bf16[4,6,128,128]{3,2,1,0:T(8,128)(2,1)S(1)} %get-tuple-element.22.remote, f32[6,128,128]{2,1,0:T(8,128)S(1)} %get-tuple-element.23.base, f32[6,8,128]{2,1,0:T(8,128)S(1)} %get-tuple-element.24.late, ...), custom_call_target="tpu_custom_call", output_to_operand_aliasing={{1}: (3, {})} | custom-call | tf_op jit(solution)/shard_map/early_slots/pallas_call | solution.py:332
  14.1 2.3 %collective-permute-done.2.ra = bf16[12,128,128]{2,1,0:T(8,128)(2,1)S(1)} collective-permute-done((bf16[12,128,128]{2,1,0:T(8,128)(2,1)S(1)}, bf16[12,128,128]{2,1,0:T(8,128)(2,1)S(1)}, u32[]{:S(2)}, u32[]{:S(2)}) %collective-permute-start.2) | collective-permute-done | bytes 393248 | tf_op jit(solution)/shard_map/ppermute | solution.py:308
  16.4 0.0 collective-permute-done.3.rb
  16.4 2.3 %second_inverses.1 = (bf16[8,128,128]{2,1,0:T(8,128)(2,1)}, bf16[8,6,128,128]{3,2,1,0:T(8,128)(2,1)}, bf16[6,5,128,128]{3,2,1,0:T(8,128)(2,1)S(1)}) custom-call(bf16[8,6,128,128]{3,2,1,0:T(8,128)(2,1)} %get-tuple-element.21.factor_in, bf16[6,5,128,128]{3,2,1,0:T(8,128)(2,1)S(1)} %get-tuple-element.28.kept_in, ...), custom_call_target="tpu_custom_call", output_to_operand_aliasing={{1}: (0, {}), {2}: (1, {})} | custom-call | tf_op jit(solution)/shard_map/second_inverses/pallas_call | solution.py:342
Async XLA Ops:
  3.1 10.4 %collective-permute-start = (bf16[12,128,128]{2,1,0:T(8,128)(2,1)S(1)}, bf16[12,128,128]{2,1,0:T(8,128)(2,1)S(1)}, u32[]{:S(2)}, u32[]{:S(2)}) collective-permute-start(bf16[12,128,128]{2,1,0:T(8,128)(2,1)S(1)} %get-tuple-element.26), channel_id=1, source_target_pairs={{0,28},{1,29},{2,30},{3,7},{4,5},{5,4},{6,10},{7,3},{8,9},{9,8},{1... | collective-permute-start | bytes 1179656 | tf_op jit(solution)/shard_map/ppermute | solution.py:308
  5.3 8.2 %collective-permute-start.1 = (bf16[12,128,128]{2,1,0:T(8,128)(2,1)S(1)}, bf16[12,128,128]{2,1,0:T(8,128)(2,1)S(1)}, u32[]{:S(2)}, u32[]{:S(2)}) collective-permute-start(bf16[12,128,128]{2,1,0:T(8,128)(2,1)S(1)} %get-tuple-element.27), channel_id=1, source_target_pairs={{0,4},{1,2},{2,1},{3,31},{4,0},{5,6},{6,5},{7,11},{8,12},{9,10},{1... | collective-permute-start | bytes 1179656 | tf_op jit(solution)/shard_map/ppermute | solution.py:308
  6.6 9.8 %collective-permute-start.2 = (bf16[12,128,128]{2,1,0:T(8,128)(2,1)S(1)}, bf16[12,128,128]{2,1,0:T(8,128)(2,1)S(1)}, u32[]{:S(2)}, u32[]{:S(2)}) collective-permute-start(bf16[12,128,128]{2,1,0:T(8,128)(2,1)S(1)} %get-tuple-element.30), channel_id=1, source_target_pairs={{0,1},{1,0},{2,3},{3,2},{4,8},{5,9},{6,7},{7,6},{8,4},{9,5},{10,14... | collective-permute-start | bytes 1179656 | tf_op jit(solution)/shard_map/ppermute | solution.py:308
  7.4 9.0 %collective-permute-start.3 = (bf16[12,128,128]{2,1,0:T(8,128)(2,1)S(1)}, bf16[12,128,128]{2,1,0:T(8,128)(2,1)S(1)}, u32[]{:S(2)}, u32[]{:S(2)}) collective-permute-start(bf16[12,128,128]{2,1,0:T(8,128)(2,1)S(1)} %get-tuple-element.31), channel_id=1, source_target_pairs={{0,4},{1,5},{2,6},{3,7},{4,0},{5,1},{6,2},{7,3},{8,12},{9,13},{10,... | collective-permute-start | bytes 1179656 | tf_op jit(solution)/shard_map/ppermute | solution.py:308

commit v6 on v5

--- a/solution.py
+++ b/solution.py
@@ -243,18 +243,15 @@
     return total - gained
 
 
-def early_kernel(capacity, arrived, remote, base, late, kept_in, ra, rb, total, kept):
-    del kept_in
-    for t in range(capacity):
-        total[t] = take(capacity, t, arrived, remote, (ra, rb), late, kept, base[t])
-
-
 def second_kernel(
-    capacity, rows, arrived, factor_in, kept_in, inverse, total, remote, late, ra, rb, pivot, factor_hbm, kept, sem,
+    capacity, rows, factor_in, kept_in, inverse, base, remote, late, r0, r1, r2, r3, pivot, factor_hbm, kept, sem,
 ):
     del factor_in, kept_in
     start = rows - capacity
-    pivots = [take(capacity, t, arrived, remote, (ra, rb), late, kept, total[t]) for t in range(capacity)]
+    pivots = []
+    for t in range(capacity):
+        left = take(capacity, t, (0, 1), remote, (r0, r1), late, kept, base[t])
+        pivots.append(take(capacity, t, (2, 3), remote, (r2, r3), late, kept, left))
     finished = kept.at[:, pl.ds(0, REMOTE)]
     copy = pltpu.make_async_copy(finished, factor_hbm.at[pl.ds(start, capacity), pl.ds(0, REMOTE)], sem)
     copy.start()
@@ -328,27 +325,16 @@
         name="local_slots",
     )(neighbors, levels, diag, off, inverse)
 
-    before, after = (0, 1), (2, 3)
-    total, kept = pl.pallas_call(
-        functools.partial(early_kernel, capacity, before),
-        out_shape=[totals, kepts],
-        in_specs=[vmem] * 6,
-        out_specs=[vmem, vmem],
-        input_output_aliases={3: 1},
-        compiler_params=params,
-        name="early_slots",
-    )(remote, base, late, kept, *(received[j] for j in before))
-
     pivot, factor, _ = pl.pallas_call(
-        functools.partial(second_kernel, capacity, rows, after),
+        functools.partial(second_kernel, capacity, rows),
         out_shape=[pivots, factors, kepts],
-        in_specs=[hbm] + [vmem] * 7,
+        in_specs=[hbm] + [vmem] * 9,
         out_specs=[vmem, hbm, vmem],
         scratch_shapes=[pltpu.SemaphoreType.DMA],
         input_output_aliases={0: 1, 1: 2},
         compiler_params=params,
         name="second_inverses",
-    )(factor, kept, inverse, total, remote, late, *(received[j] for j in after))
+    )(factor, kept, inverse, base, remote, late, *received)
     return (pivot, factor)
 
 

time: 18.9 us -> 19 us (level)
  waiting for transfers between devices: 2.33 us -> 2.81 us
  Pallas kernels: 9.09 us -> 8.69 us
    ppermute x4, waiting for transfers between devices: 2.33 us -> 2.81 us  [shards(): lax.ppermute(payloads[j], ('row', 'col'), steps[j])]
    pallas_call x2 -> x1, Pallas kernels: 2.77 us -> 2.38 us  [shards(): pl.pallas_call(functools.partial(second_kernel, capacity, rows), out_shap...]
  transfers between devices with their start and end apart: 4 -> 4, of which waited for: 1 -> 1; matrix products, arithmetic and copies ran while one was open for 0% -> 0% of each run, Pallas kernels for 23% -> 20%
where the time goes in v6:
time: 19 us; the launch traced here: 18.8 us
  Pallas kernels  8.69 us (46%)
  starting transfers between devices  6.61 us (35%)
  waiting for transfers between devices  2.81 us (15%)
  between operations  0.66 us (3%)
    ppermute x4, starting transfers between devices, shards(): lax.ppermute(payloads[j], ('row', 'col'), steps[j])  6.61 us
    pallas_call x1, Pallas kernels, shards(): pl.pallas_call(functools.partial(local_kernel, capacity, rows), out_shape...  3.82 us
    ppermute x4, waiting for transfers between devices, shards(): lax.ppermute(payloads[j], ('row', 'col'), steps[j])  2.81 us
    pallas_call x1, Pallas kernels, shards(): pl.pallas_call(functools.partial(first_kernel, capacity, rows), out_shape...  2.5 us
    pallas_call x1, Pallas kernels, shards(): pl.pallas_call(functools.partial(second_kernel, capacity, rows), out_shap...  2.38 us
  transfers between devices with their start and end apart: 4, of which 1 were waited for; matrix products, arithmetic and copies ran while one was open for 0% of the time, Pallas kernels for 20%

profile of v6, /device:TPU:1, one launch (start us, length us, event | category | flops | bytes accessed | tf_op | source)
XLA Modules:
  0.0 18.8 jit_solution(4059851202621056693)
XLA Ops:
  0.6 2.5 %first_inverses.1 = (bf16[12,128,128]{2,1,0:T(8,128)(2,1)S(1)}, bf16[12,128,128]{2,1,0:T(8,128)(2,1)S(1)}, bf16[12,128,128]{2,1,0:T(8,128)(2,1)S(1)}, bf16[12,12...) custom-call(s32[8,6]{1,0:T(8,128)} %neighbors.1, ...), custom_call_target="tpu_custom_call" | custom-call | tf_op jit(solution)/shard_map/first_inverses/pallas_call | solution.py:289
  3.1 2.2 %collective-permute-start = (bf16[12,128,128]{2,1,0:T(8,128)(2,1)S(1)}, bf16[12,128,128]{2,1,0:T(8,128)(2,1)S(1)}, u32[]{:S(2)}, u32[]{:S(2)}) collective-permute-start(bf16[12,128,128]{2,1,0:T(8,128)(2,1)S(1)} %get-tuple-element.24), channel_id=1, source_target_pairs={{0,28},{1,29},{2,30},{3,7},{4,5},{5,4},{6,10},{7,3},{8,9},{9,8},{1... | collective-permute-start | bytes 1179656 | tf_op jit(solution)/shard_map/ppermute | solution.py:305
  5.3 1.3 %collective-permute-start.1 = (bf16[12,128,128]{2,1,0:T(8,128)(2,1)S(1)}, bf16[12,128,128]{2,1,0:T(8,128)(2,1)S(1)}, u32[]{:S(2)}, u32[]{:S(2)}) collective-permute-start(bf16[12,128,128]{2,1,0:T(8,128)(2,1)S(1)} %get-tuple-element.25), channel_id=1, source_target_pairs={{0,4},{1,2},{2,1},{3,31},{4,0},{5,6},{6,5},{7,11},{8,12},{9,10},{1... | collective-permute-start | bytes 1179656 | tf_op jit(solution)/shard_map/ppermute | solution.py:305
  6.6 0.8 %collective-permute-start.2 = (bf16[12,128,128]{2,1,0:T(8,128)(2,1)S(1)}, bf16[12,128,128]{2,1,0:T(8,128)(2,1)S(1)}, u32[]{:S(2)}, u32[]{:S(2)}) collective-permute-start(bf16[12,128,128]{2,1,0:T(8,128)(2,1)S(1)} %get-tuple-element.26), channel_id=1, source_target_pairs={{0,1},{1,0},{2,3},{3,2},{4,8},{5,9},{6,7},{7,6},{8,4},{9,5},{10,14... | collective-permute-start | bytes 1179656 | tf_op jit(solution)/shard_map/ppermute | solution.py:305
  7.4 2.3 %collective-permute-start.3 = (bf16[12,128,128]{2,1,0:T(8,128)(2,1)S(1)}, bf16[12,128,128]{2,1,0:T(8,128)(2,1)S(1)}, u32[]{:S(2)}, u32[]{:S(2)}) collective-permute-start(bf16[12,128,128]{2,1,0:T(8,128)(2,1)S(1)} %get-tuple-element.27), channel_id=1, source_target_pairs={{0,4},{1,5},{2,6},{3,7},{4,0},{5,1},{6,2},{7,3},{8,12},{9,13},{10,... | collective-permute-start | bytes 1179656 | tf_op jit(solution)/shard_map/ppermute | solution.py:305
  9.7 3.8 %local_slots.1 = (bf16[8,6,128,128]{3,2,1,0:T(8,128)(2,1)}, f32[6,128,128]{2,1,0:T(8,128)S(1)}, bf16[4,6,128,128]{3,2,1,0:T(8,128)(2,1)S(1)}, bf16[6,5,128,128]{3,2,1,0:T(8,128)(2,1)S(1)}, f32[6,8,128]{2,1,0:T(8,128)S(1)}) custom-call(s32[8,6]{1,0:T(8,128)} %neighbors.1, s32[8]{0:T(128)} %levels.1, bf16[8,128,128]{2,1,0:T(8,128)(2,1)S(1)} %get-tuple-element.16.diag, ...), custom_call_target="tpu_custom_call" | custom-call | flops 400000000 | bytes 4000000 | tf_op jit(solution)/shard_map/local_slots/pallas_call | solution.py:307
  13.6 0.0 collective-permute-done.r0
  13.6 0.0 collective-permute-done.1.r1
  13.6 2.8 %collective-permute-done.2.r2 = bf16[12,128,128]{2,1,0:T(8,128)(2,1)S(1)} collective-permute-done((bf16[12,128,128]{2,1,0:T(8,128)(2,1)S(1)}, bf16[12,128,128]{2,1,0:T(8,128)(2,1)S(1)}, u32[]{:S(2)}, u32[]{:S(2)}) %collective-permute-start.2) | collective-permute-done | bytes 393248 | tf_op jit(solution)/shard_map/ppermute | solution.py:305
  16.4 0.0 collective-permute-done.3.r3
  16.4 2.4 %second_inverses.1 = (bf16[8,128,128]{2,1,0:T(8,128)(2,1)}, bf16[8,6,128,128]{3,2,1,0:T(8,128)(2,1)}, bf16[6,5,128,128]{3,2,1,0:T(8,128)(2,1)S(1)}) custom-call(bf16[8,6,128,128]{3,2,1,0:T(8,128)(2,1)} %get-tuple-element.19.factor_in, bf16[6,5,128,128]{3,2,1,0:T(8,128)(2,1)S(1)} %get-tuple-element.20.kept_in, ...), custom_call_target="tpu_custom_call", output_to_operand_aliasing={{1}: (0, {}), {2}: (1, {})} | custom-call | tf_op jit(solution)/shard_map/second_inverses/pallas_call | solution.py:328
Async XLA Ops:
  3.1 10.4 %collective-permute-start = (bf16[12,128,128]{2,1,0:T(8,128)(2,1)S(1)}, bf16[12,128,128]{2,1,0:T(8,128)(2,1)S(1)}, u32[]{:S(2)}, u32[]{:S(2)}) collective-permute-start(bf16[12,128,128]{2,1,0:T(8,128)(2,1)S(1)} %get-tuple-element.24), channel_id=1, source_target_pairs={{0,28},{1,29},{2,30},{3,7},{4,5},{5,4},{6,10},{7,3},{8,9},{9,8},{1... | collective-permute-start | bytes 1179656 | tf_op jit(solution)/shard_map/ppermute | solution.py:305
  5.3 8.2 %collective-permute-start.1 = (bf16[12,128,128]{2,1,0:T(8,128)(2,1)S(1)}, bf16[12,128,128]{2,1,0:T(8,128)(2,1)S(1)}, u32[]{:S(2)}, u32[]{:S(2)}) collective-permute-start(bf16[12,128,128]{2,1,0:T(8,128)(2,1)S(1)} %get-tuple-element.25), channel_id=1, source_target_pairs={{0,4},{1,2},{2,1},{3,31},{4,0},{5,6},{6,5},{7,11},{8,12},{9,10},{1... | collective-permute-start | bytes 1179656 | tf_op jit(solution)/shard_map/ppermute | solution.py:305
  6.6 9.8 %collective-permute-start.2 = (bf16[12,128,128]{2,1,0:T(8,128)(2,1)S(1)}, bf16[12,128,128]{2,1,0:T(8,128)(2,1)S(1)}, u32[]{:S(2)}, u32[]{:S(2)}) collective-permute-start(bf16[12,128,128]{2,1,0:T(8,128)(2,1)S(1)} %get-tuple-element.26), channel_id=1, source_target_pairs={{0,1},{1,0},{2,3},{3,2},{4,8},{5,9},{6,7},{7,6},{8,4},{9,5},{10,14... | collective-permute-start | bytes 1179656 | tf_op jit(solution)/shard_map/ppermute | solution.py:305
  7.4 9.0 %collective-permute-start.3 = (bf16[12,128,128]{2,1,0:T(8,128)(2,1)S(1)}, bf16[12,128,128]{2,1,0:T(8,128)(2,1)S(1)}, u32[]{:S(2)}, u32[]{:S(2)}) collective-permute-start(bf16[12,128,128]{2,1,0:T(8,128)(2,1)S(1)} %get-tuple-element.27), channel_id=1, source_target_pairs={{0,4},{1,5},{2,6},{3,7},{4,0},{5,1},{6,2},{7,3},{8,12},{9,13},{10,... | collective-permute-start | bytes 1179656 | tf_op jit(solution)/shard_map/ppermute | solution.py:305

commit v7 on v6

--- a/solution.py
+++ b/solution.py
@@ -11,14 +11,14 @@
 VMEM_LIMIT = 40 * 1024 * 1024
 REMOTE = 4
 EVERY_DEVICE = (
-    ((6, 0, 2, 4), (6, 2, 3, 0), (6, 3, 2, 0), (0, 6, 3, 4)),
-    ((2, 1, 0, 5), (3, 2, 0, 1), (0, 3, 2, 1), (1, 0, 3, 5)),
-    ((2, 0, 1, 4), (3, 2, 1, 0), (1, 3, 0, 2), (0, 1, 4, 3)),
-    ((0, 1, 2, 5), (0, 2, 3, 1), (0, 3, 1, 2), (1, 0, 5, 3)),
+    ((6, 0, 4, 2), (6, 2, 0, 3), (6, 3, 2, 0), (0, 6, 3, 4)),
+    ((2, 1, 5, 0), (3, 2, 1, 0), (0, 3, 2, 1), (1, 0, 3, 5)),
+    ((2, 4, 0, 1), (3, 2, 0, 1), (1, 3, 2, 0), (0, 1, 3, 4)),
+    ((0, 5, 1, 2), (0, 2, 1, 3), (0, 3, 2, 1), (1, 0, 3, 5)),
     ((1, 2, 4, 0), (1, 3, 2, 0), (1, 0, 3, 2), (0, 1, 4, 3)),
     ((0, 2, 5, 1), (0, 3, 2, 1), (0, 1, 3, 2), (1, 0, 5, 3)),
-    ((1, 0, 2, 4), (1, 2, 3, 0), (1, 3, 2, 0), (4, 1, 3, 0)),
-    ((6, 1, 2, 5), (6, 2, 3, 1), (6, 3, 2, 1), (5, 6, 3, 1)),
+    ((1, 4, 2, 0), (1, 2, 3, 0), (1, 3, 0, 2), (4, 1, 0, 3)),
+    ((6, 5, 2, 1), (6, 2, 3, 1), (6, 3, 1, 2), (5, 6, 1, 3)),
 )
 ANY_MESH = (
     ((2, 1, 3, 0), (3, 1, 2, 0)),

time: 19 us -> 19 us (level)
  starting transfers between devices: 6.61 us -> 4.76 us
  waiting for transfers between devices: 2.81 us -> 4.65 us
    ppermute x4, starting transfers between devices: 6.61 us -> 4.76 us  [shards(): lax.ppermute(payloads[j], ('row', 'col'), steps[j])]
    ppermute x4, waiting for transfers between devices: 2.81 us -> 4.65 us  [shards(): lax.ppermute(payloads[j], ('row', 'col'), steps[j])]
where the time goes in v7:
time: 19 us; the launch traced here: 18.8 us
  Pallas kernels  8.69 us (46%)
  starting transfers between devices  4.76 us (25%)
  waiting for transfers between devices  4.65 us (24%)
  between operations  0.67 us (4%)
    ppermute x4, starting transfers between devices, shards(): lax.ppermute(payloads[j], ('row', 'col'), steps[j])  4.76 us
    ppermute x4, waiting for transfers between devices, shards(): lax.ppermute(payloads[j], ('row', 'col'), steps[j])  4.65 us
    pallas_call x1, Pallas kernels, shards(): pl.pallas_call(functools.partial(local_kernel, capacity, rows), out_shape...  3.82 us
    pallas_call x1, Pallas kernels, shards(): pl.pallas_call(functools.partial(first_kernel, capacity, rows), out_shape...  2.5 us
    pallas_call x1, Pallas kernels, shards(): pl.pallas_call(functools.partial(second_kernel, capacity, rows), out_shap...  2.37 us
  transfers between devices with their start and end apart: 4, of which 1 were waited for; matrix products, arithmetic and copies ran while one was open for 0% of the time, Pallas kernels for 20%

profile of v7, /device:TPU:1, one launch (start us, length us, event | category | flops | bytes accessed | tf_op | source)
XLA Modules:
  0.0 18.8 jit_solution(1790042118651771243)
XLA Ops:
  0.6 2.5 %first_inverses.1 = (bf16[12,128,128]{2,1,0:T(8,128)(2,1)S(1)}, bf16[12,128,128]{2,1,0:T(8,128)(2,1)S(1)}, bf16[12,128,128]{2,1,0:T(8,128)(2,1)S(1)}, bf16[12,12...) custom-call(s32[8,6]{1,0:T(8,128)} %neighbors.1, ...), custom_call_target="tpu_custom_call" | custom-call | tf_op jit(solution)/shard_map/first_inverses/pallas_call | solution.py:289
  3.1 2.2 %collective-permute-start = (bf16[12,128,128]{2,1,0:T(8,128)(2,1)S(1)}, bf16[12,128,128]{2,1,0:T(8,128)(2,1)S(1)}, u32[]{:S(2)}, u32[]{:S(2)}) collective-permute-start(bf16[12,128,128]{2,1,0:T(8,128)(2,1)S(1)} %get-tuple-element.24), channel_id=1, source_target_pairs={{0,28},{1,29},{2,30},{3,7},{4,5},{5,4},{6,10},{7,3},{8,9},{9,8},{1... | collective-permute-start | bytes 1179656 | tf_op jit(solution)/shard_map/ppermute | solution.py:305
  5.3 1.3 %collective-permute-start.1 = (bf16[12,128,128]{2,1,0:T(8,128)(2,1)S(1)}, bf16[12,128,128]{2,1,0:T(8,128)(2,1)S(1)}, u32[]{:S(2)}, u32[]{:S(2)}) collective-permute-start(bf16[12,128,128]{2,1,0:T(8,128)(2,1)S(1)} %get-tuple-element.25), channel_id=1, source_target_pairs={{0,4},{1,2},{2,1},{3,31},{4,0},{5,6},{6,5},{7,11},{8,12},{9,10},{1... | collective-permute-start | bytes 1179656 | tf_op jit(solution)/shard_map/ppermute | solution.py:305
  6.6 0.0 collective-permute-start.2
  6.6 1.3 %collective-permute-start.3 = (bf16[12,128,128]{2,1,0:T(8,128)(2,1)S(1)}, bf16[12,128,128]{2,1,0:T(8,128)(2,1)S(1)}, u32[]{:S(2)}, u32[]{:S(2)}) collective-permute-start(bf16[12,128,128]{2,1,0:T(8,128)(2,1)S(1)} %get-tuple-element.27), channel_id=1, source_target_pairs={{0,1},{1,0},{2,6},{3,7},{4,8},{5,9},{6,2},{7,3},{8,4},{9,5},{10,14... | collective-permute-start | bytes 1179656 | tf_op jit(solution)/shard_map/ppermute | solution.py:305
  7.9 3.8 %local_slots.1 = (bf16[8,6,128,128]{3,2,1,0:T(8,128)(2,1)}, f32[6,128,128]{2,1,0:T(8,128)S(1)}, bf16[4,6,128,128]{3,2,1,0:T(8,128)(2,1)S(1)}, bf16[6,5,128,128]{3,2,1,0:T(8,128)(2,1)S(1)}, f32[6,8,128]{2,1,0:T(8,128)S(1)}) custom-call(s32[8,6]{1,0:T(8,128)} %neighbors.1, s32[8]{0:T(128)} %levels.1, bf16[8,128,128]{2,1,0:T(8,128)(2,1)S(1)} %get-tuple-element.16.diag, ...), custom_call_target="tpu_custom_call" | custom-call | flops 400000000 | bytes 4000000 | tf_op jit(solution)/shard_map/local_slots/pallas_call | solution.py:307
  11.7 0.0 collective-permute-done.r0
  11.7 0.0 collective-permute-done.1.r1
  11.8 0.0 collective-permute-done.2.r2
  11.8 4.6 %collective-permute-done.3.r3 = bf16[12,128,128]{2,1,0:T(8,128)(2,1)S(1)} collective-permute-done((bf16[12,128,128]{2,1,0:T(8,128)(2,1)S(1)}, bf16[12,128,128]{2,1,0:T(8,128)(2,1)S(1)}, u32[]{:S(2)}, u32[]{:S(2)}) %collective-permute-start.3) | collective-permute-done | bytes 393248 | tf_op jit(solution)/shard_map/ppermute | solution.py:305
  16.4 2.4 %second_inverses.1 = (bf16[8,128,128]{2,1,0:T(8,128)(2,1)}, bf16[8,6,128,128]{3,2,1,0:T(8,128)(2,1)}, bf16[6,5,128,128]{3,2,1,0:T(8,128)(2,1)S(1)}) custom-call(bf16[8,6,128,128]{3,2,1,0:T(8,128)(2,1)} %get-tuple-element.19.factor_in, bf16[6,5,128,128]{3,2,1,0:T(8,128)(2,1)S(1)} %get-tuple-element.20.kept_in, ...), custom_call_target="tpu_custom_call", output_to_operand_aliasing={{1}: (0, {}), {2}: (1, {})} | custom-call | tf_op jit(solution)/shard_map/second_inverses/pallas_call | solution.py:328
Async XLA Ops:
  3.1 8.6 %collective-permute-start = (bf16[12,128,128]{2,1,0:T(8,128)(2,1)S(1)}, bf16[12,128,128]{2,1,0:T(8,128)(2,1)S(1)}, u32[]{:S(2)}, u32[]{:S(2)}) collective-permute-start(bf16[12,128,128]{2,1,0:T(8,128)(2,1)S(1)} %get-tuple-element.24), channel_id=1, source_target_pairs={{0,28},{1,29},{2,30},{3,7},{4,5},{5,4},{6,10},{7,3},{8,9},{9,8},{1... | collective-permute-start | bytes 1179656 | tf_op jit(solution)/shard_map/ppermute | solution.py:305
  5.3 6.4 %collective-permute-start.1 = (bf16[12,128,128]{2,1,0:T(8,128)(2,1)S(1)}, bf16[12,128,128]{2,1,0:T(8,128)(2,1)S(1)}, u32[]{:S(2)}, u32[]{:S(2)}) collective-permute-start(bf16[12,128,128]{2,1,0:T(8,128)(2,1)S(1)} %get-tuple-element.25), channel_id=1, source_target_pairs={{0,4},{1,2},{2,1},{3,31},{4,0},{5,6},{6,5},{7,11},{8,12},{9,10},{1... | collective-permute-start | bytes 1179656 | tf_op jit(solution)/shard_map/ppermute | solution.py:305
  6.6 5.1 %collective-permute-start.2 = (bf16[12,128,128]{2,1,0:T(8,128)(2,1)S(1)}, bf16[12,128,128]{2,1,0:T(8,128)(2,1)S(1)}, u32[]{:S(2)}, u32[]{:S(2)}) collective-permute-start(bf16[12,128,128]{2,1,0:T(8,128)(2,1)S(1)} %get-tuple-element.26), channel_id=1, source_target_pairs={{0,4},{1,5},{2,3},{3,2},{4,0},{5,1},{6,7},{7,6},{8,12},{9,13},{10,... | collective-permute-start | bytes 1179656 | tf_op jit(solution)/shard_map/ppermute | solution.py:305
  6.6 9.8 %collective-permute-start.3 = (bf16[12,128,128]{2,1,0:T(8,128)(2,1)S(1)}, bf16[12,128,128]{2,1,0:T(8,128)(2,1)S(1)}, u32[]{:S(2)}, u32[]{:S(2)}) collective-permute-start(bf16[12,128,128]{2,1,0:T(8,128)(2,1)S(1)} %get-tuple-element.27), channel_id=1, source_target_pairs={{0,1},{1,0},{2,6},{3,7},{4,8},{5,9},{6,2},{7,3},{8,4},{9,5},{10,14... | collective-permute-start | bytes 1179656 | tf_op jit(solution)/shard_map/ppermute | solution.py:305

commit v8 on v7

--- a/solution.py
+++ b/solution.py
@@ -230,8 +230,7 @@
     each(lambda c: c.wait())
 
 
-def take(capacity, t, arrived, remote, received, late, kept, total):
-    order = slot_order()
+def take(capacity, order, t, arrived, remote, received, late, kept, total):
     lowers, gained = pair_sums(
         [remote[j, t] for j in arrived],
         [blocks[t] for blocks in received],
@@ -248,10 +247,11 @@
 ):
     del factor_in, kept_in
     start = rows - capacity
+    order = slot_order()
     pivots = []
     for t in range(capacity):
-        left = take(capacity, t, (0, 1), remote, (r0, r1), late, kept, base[t])
-        pivots.append(take(capacity, t, (2, 3), remote, (r2, r3), late, kept, left))
+        left = take(capacity, order, t, (0, 1), remote, (r0, r1), late, kept, base[t])
+        pivots.append(take(capacity, order, t, (2, 3), remote, (r2, r3), late, kept, left))
     finished = kept.at[:, pl.ds(0, REMOTE)]
     copy = pltpu.make_async_copy(finished, factor_hbm.at[pl.ds(start, capacity), pl.ds(0, REMOTE)], sem)
     copy.start()

time: 19 us -> 19 us (level)
  no operation moved by 1% of the time
where the time goes in v8:
time: 19 us; the launch traced here: 18.8 us
  Pallas kernels  8.69 us (46%)
  starting transfers between devices  4.76 us (25%)
  waiting for transfers between devices  4.65 us (24%)
  between operations  0.67 us (4%)
    ppermute x4, starting transfers between devices, shards(): lax.ppermute(payloads[j], ('row', 'col'), steps[j])  4.76 us
    ppermute x4, waiting for transfers between devices, shards(): lax.ppermute(payloads[j], ('row', 'col'), steps[j])  4.65 us
    pallas_call x1, Pallas kernels, shards(): pl.pallas_call(functools.partial(local_kernel, capacity, rows), out_shape...  3.82 us
    pallas_call x1, Pallas kernels, shards(): pl.pallas_call(functools.partial(first_kernel, capacity, rows), out_shape...  2.5 us
    pallas_call x1, Pallas kernels, shards(): pl.pallas_call(functools.partial(second_kernel, capacity, rows), out_shap...  2.37 us
  transfers between devices with their start and end apart: 4, of which 1 were waited for; matrix products, arithmetic and copies ran while one was open for 0% of the time, Pallas kernels for 20%

profile of v8, /device:TPU:1, one launch (start us, length us, event | category | flops | bytes accessed | tf_op | source)
XLA Modules:
  0.0 18.8 jit_solution(1790042118651771243)
XLA Ops:
  0.6 2.5 %first_inverses.1 = (bf16[12,128,128]{2,1,0:T(8,128)(2,1)S(1)}, bf16[12,128,128]{2,1,0:T(8,128)(2,1)S(1)}, bf16[12,128,128]{2,1,0:T(8,128)(2,1)S(1)}, bf16[12,12...) custom-call(s32[8,6]{1,0:T(8,128)} %neighbors.1, ...), custom_call_target="tpu_custom_call" | custom-call | tf_op jit(solution)/shard_map/first_inverses/pallas_call | solution.py:289
  3.1 2.2 %collective-permute-start = (bf16[12,128,128]{2,1,0:T(8,128)(2,1)S(1)}, bf16[12,128,128]{2,1,0:T(8,128)(2,1)S(1)}, u32[]{:S(2)}, u32[]{:S(2)}) collective-permute-start(bf16[12,128,128]{2,1,0:T(8,128)(2,1)S(1)} %get-tuple-element.24), channel_id=1, source_target_pairs={{0,28},{1,29},{2,30},{3,7},{4,5},{5,4},{6,10},{7,3},{8,9},{9,8},{1... | collective-permute-start | bytes 1179656 | tf_op jit(solution)/shard_map/ppermute | solution.py:305
  5.3 1.3 %collective-permute-start.1 = (bf16[12,128,128]{2,1,0:T(8,128)(2,1)S(1)}, bf16[12,128,128]{2,1,0:T(8,128)(2,1)S(1)}, u32[]{:S(2)}, u32[]{:S(2)}) collective-permute-start(bf16[12,128,128]{2,1,0:T(8,128)(2,1)S(1)} %get-tuple-element.25), channel_id=1, source_target_pairs={{0,4},{1,2},{2,1},{3,31},{4,0},{5,6},{6,5},{7,11},{8,12},{9,10},{1... | collective-permute-start | bytes 1179656 | tf_op jit(solution)/shard_map/ppermute | solution.py:305
  6.6 0.0 collective-permute-start.2
  6.6 1.3 %collective-permute-start.3 = (bf16[12,128,128]{2,1,0:T(8,128)(2,1)S(1)}, bf16[12,128,128]{2,1,0:T(8,128)(2,1)S(1)}, u32[]{:S(2)}, u32[]{:S(2)}) collective-permute-start(bf16[12,128,128]{2,1,0:T(8,128)(2,1)S(1)} %get-tuple-element.27), channel_id=1, source_target_pairs={{0,1},{1,0},{2,6},{3,7},{4,8},{5,9},{6,2},{7,3},{8,4},{9,5},{10,14... | collective-permute-start | bytes 1179656 | tf_op jit(solution)/shard_map/ppermute | solution.py:305
  7.9 3.8 %local_slots.1 = (bf16[8,6,128,128]{3,2,1,0:T(8,128)(2,1)}, f32[6,128,128]{2,1,0:T(8,128)S(1)}, bf16[4,6,128,128]{3,2,1,0:T(8,128)(2,1)S(1)}, bf16[6,5,128,128]{3,2,1,0:T(8,128)(2,1)S(1)}, f32[6,8,128]{2,1,0:T(8,128)S(1)}) custom-call(s32[8,6]{1,0:T(8,128)} %neighbors.1, s32[8]{0:T(128)} %levels.1, bf16[8,128,128]{2,1,0:T(8,128)(2,1)S(1)} %get-tuple-element.16.diag, ...), custom_call_target="tpu_custom_call" | custom-call | flops 400000000 | bytes 4000000 | tf_op jit(solution)/shard_map/local_slots/pallas_call | solution.py:307
  11.7 0.0 collective-permute-done.r0
  11.7 0.0 collective-permute-done.1.r1
  11.8 0.0 collective-permute-done.2.r2
  11.8 4.6 %collective-permute-done.3.r3 = bf16[12,128,128]{2,1,0:T(8,128)(2,1)S(1)} collective-permute-done((bf16[12,128,128]{2,1,0:T(8,128)(2,1)S(1)}, bf16[12,128,128]{2,1,0:T(8,128)(2,1)S(1)}, u32[]{:S(2)}, u32[]{:S(2)}) %collective-permute-start.3) | collective-permute-done | bytes 393248 | tf_op jit(solution)/shard_map/ppermute | solution.py:305
  16.4 2.4 %second_inverses.1 = (bf16[8,128,128]{2,1,0:T(8,128)(2,1)}, bf16[8,6,128,128]{3,2,1,0:T(8,128)(2,1)}, bf16[6,5,128,128]{3,2,1,0:T(8,128)(2,1)S(1)}) custom-call(bf16[8,6,128,128]{3,2,1,0:T(8,128)(2,1)} %get-tuple-element.19.factor_in, bf16[6,5,128,128]{3,2,1,0:T(8,128)(2,1)S(1)} %get-tuple-element.20.kept_in, ...), custom_call_target="tpu_custom_call", output_to_operand_aliasing={{1}: (0, {}), {2}: (1, {})} | custom-call | tf_op jit(solution)/shard_map/second_inverses/pallas_call | solution.py:328
Async XLA Ops:
  3.1 8.6 %collective-permute-start = (bf16[12,128,128]{2,1,0:T(8,128)(2,1)S(1)}, bf16[12,128,128]{2,1,0:T(8,128)(2,1)S(1)}, u32[]{:S(2)}, u32[]{:S(2)}) collective-permute-start(bf16[12,128,128]{2,1,0:T(8,128)(2,1)S(1)} %get-tuple-element.24), channel_id=1, source_target_pairs={{0,28},{1,29},{2,30},{3,7},{4,5},{5,4},{6,10},{7,3},{8,9},{9,8},{1... | collective-permute-start | bytes 1179656 | tf_op jit(solution)/shard_map/ppermute | solution.py:305
  5.3 6.4 %collective-permute-start.1 = (bf16[12,128,128]{2,1,0:T(8,128)(2,1)S(1)}, bf16[12,128,128]{2,1,0:T(8,128)(2,1)S(1)}, u32[]{:S(2)}, u32[]{:S(2)}) collective-permute-start(bf16[12,128,128]{2,1,0:T(8,128)(2,1)S(1)} %get-tuple-element.25), channel_id=1, source_target_pairs={{0,4},{1,2},{2,1},{3,31},{4,0},{5,6},{6,5},{7,11},{8,12},{9,10},{1... | collective-permute-start | bytes 1179656 | tf_op jit(solution)/shard_map/ppermute | solution.py:305
  6.6 5.1 %collective-permute-start.2 = (bf16[12,128,128]{2,1,0:T(8,128)(2,1)S(1)}, bf16[12,128,128]{2,1,0:T(8,128)(2,1)S(1)}, u32[]{:S(2)}, u32[]{:S(2)}) collective-permute-start(bf16[12,128,128]{2,1,0:T(8,128)(2,1)S(1)} %get-tuple-element.26), channel_id=1, source_target_pairs={{0,4},{1,5},{2,3},{3,2},{4,0},{5,1},{6,7},{7,6},{8,12},{9,13},{10,... | collective-permute-start | bytes 1179656 | tf_op jit(solution)/shard_map/ppermute | solution.py:305
  6.6 9.8 %collective-permute-start.3 = (bf16[12,128,128]{2,1,0:T(8,128)(2,1)S(1)}, bf16[12,128,128]{2,1,0:T(8,128)(2,1)S(1)}, u32[]{:S(2)}, u32[]{:S(2)}) collective-permute-start(bf16[12,128,128]{2,1,0:T(8,128)(2,1)S(1)} %get-tuple-element.27), channel_id=1, source_target_pairs={{0,1},{1,0},{2,6},{3,7},{4,8},{5,9},{6,2},{7,3},{8,4},{9,5},{10,14... | collective-permute-start | bytes 1179656 | tf_op jit(solution)/shard_map/ppermute | solution.py:305
